TPU v7x, 32 devices: a whole 2x2x4 slice. The times are simulated.
32 devices in a mesh: site: 4 (over y, core), blk: 8 (over z, x).
Axes of the slice: x: 2, y: 2, z: 4, core: 2. Of those that a mesh axis runs over, the one named last changes fastest.
Arguments:
- corner: bfloat16 [4, 48, 128, 128], P('site', 'blk')
- bcorner: bfloat16 [2, 4, 48, 128, 128], P(None, 'site', 'blk'), may hold values from -6 to 6
- edge: bfloat16 [4, 48, 128, 2304], P('site', 'blk'), may hold values from -0.5 to 0.5
- bedge: bfloat16 [4, 48, 128, 2304], P('site', 'blk'), may hold values from -0.5 to 0.5
- proj: bfloat16 [4, 48, 2304, 128], P('site', 'blk'), may hold values from -0.125 to 0.125
- joining: int32 [4, 48], P('site'), may hold values from 0 to 47, as said below
- momentum: float32 [1], replicated, may hold values from 0.5 to 2.5
Outputs:
- new_corner: bfloat16 [4, 48, 128, 128], P('site', 'blk')
- new_bcorner: bfloat16 [2, 4, 48, 128, 128], P(None, 'site', 'blk')
- momentum_sum: float32 [2, 48, 128, 128], P(None, 'blk', 'site')
Inputs may be any that keep to these rules, and one draw needn't show every extreme that they name: Each row of joining is a permutation of the 48 slots. The 6 new slots of one blk device take their blocks from the slots of at most 3 blk devices, exactly 2 from each of them.
All inputs are finite; a program needn't handle non-finite values. Where the computation divides by a largest or mean magnitude, that divisor is 1e-20 or more.
Results may differ from a plain program's by a relative error of at most 0.024.
Values may be sent and summed in bfloat16 or wider, within the bound.
No kernel may reach another device: no remote copies, remote signals or barrier semaphores. Data moves between devices by JAX's collectives and lax.ppermute only.
A program may use at most 128 MiB of HBM per device.

v0:
```python
import functools

import jax
import jax.numpy as jnp
from jax import lax
from jax.experimental import pallas as pl
from jax.experimental.pallas import tpu as pltpu
from jax.sharding import PartitionSpec as P

epsilon = 1e-06
TILE = 16
SITE_STEPS = (0, 2, 3, 1)
FIRST = (6, 4, 7)
AHEAD = 2
VMEM = pl.BlockSpec(memory_space=pltpu.VMEM)
ANY = pl.BlockSpec(memory_space=pl.ANY)
HBM = pl.BlockSpec(memory_space=pltpu.HBM)


def start_order(n):
    far = sorted(range(n // 2, n), key=lambda k: (k & 1, -k))
    return (0, far[0], 1, *far[1:], *range(2, n // 2))


def my_place():
    return lax.axis_index("blk"), lax.axis_index("site")


def piece_start(j, m, n, sites):
    return pl.multiple_of(lax.rem(j, sites) * (m // sites) + lax.div(j, sites) * (m // n), m // n)


def all_swapped(parts, steps, axis):
    n = len(parts)
    return [lax.ppermute(part, axis, [(i, i ^ k) for i in range(n)]) if k else part for part, k in zip(parts, steps)]


def edge_proj_kernel(edge, bedge, proj, wv_ref, edge_buf, bedge_buf, proj_buf, sems):
    slots = proj.shape[1]
    pairs = ((proj, proj_buf), (edge, edge_buf), (bedge, bedge_buf))
    copies = [
        [pltpu.make_async_copy(src.at[0, i], buf.at[i], sems.at[3 * i + a]) for a, (src, buf) in enumerate(pairs)]
        for i in range(slots)
    ]
    for group in copies[:AHEAD]:
        for copy in group:
            copy.start()
    dot = functools.partial(jnp.dot, preferred_element_type=jnp.float32)
    for i, (first, second, third) in enumerate(copies):
        for group in copies[i + AHEAD : i + AHEAD + 1]:
            for copy in group:
                copy.start()
        first.wait()
        second.wait()
        wv_ref[2 * i] = dot(edge_buf[i], proj_buf[i]).astype(wv_ref.dtype)
        third.wait()
        wv_ref[2 * i + 1] = dot(bedge_buf[i], proj_buf[i]).astype(wv_ref.dtype)


def edge_proj(edge, bedge, proj):
    _, slots, m, k = edge.shape
    return pl.pallas_call(
        edge_proj_kernel,
        out_shape=jax.ShapeDtypeStruct((2 * slots, m, m), jnp.bfloat16),
        in_specs=[HBM] * 3,
        out_specs=VMEM,
        scratch_shapes=[
            pltpu.VMEM((slots, m, k), jnp.bfloat16),
            pltpu.VMEM((slots, m, k), jnp.bfloat16),
            pltpu.VMEM((slots, k, m), jnp.bfloat16),
            pltpu.SemaphoreType.DMA((3 * slots,)),
        ],
        cost_estimate=pl.CostEstimate(
            flops=4 * slots * m * k * m, bytes_accessed=6 * slots * m * k, transcendentals=0
        ),
        compiler_params=pltpu.CompilerParams(vmem_limit_bytes=52 << 20),
        name="edge_proj",
    )(edge, bedge, proj)


def small_call(kernel, out_shape, in_specs, scratch, name):
    return pl.pallas_call(
        kernel,
        out_shape=out_shape,
        in_specs=in_specs,
        out_specs=jax.tree.map(lambda _: VMEM, out_shape),
        scratch_shapes=scratch,
        cost_estimate=pl.CostEstimate(flops=1 << 28, bytes_accessed=1 << 20, transcendentals=0),
        compiler_params=pltpu.CompilerParams(vmem_limit_bytes=24 << 20),
        name=name,
    )


def blocks_of(turn, corner, bcorner, w, v):
    cosine, sine = turn
    dot = functools.partial(jnp.dot, preferred_element_type=jnp.float32)
    ground = dot(corner, w).astype(jnp.bfloat16)
    real_term = dot(bcorner[0], w)
    imag_term = dot(bcorner[1], w)
    re = cosine * real_term - sine * imag_term + dot(corner, v)
    im = sine * real_term + cosine * imag_term
    return ground, re.astype(jnp.bfloat16), im.astype(jnp.bfloat16)


def spread_kernel(steps, sites, turn, corner, bcorner, wv, *refs):
    n = len(steps)
    out, stage = refs[:n], refs[n]
    here = my_place()
    slots, m = corner.shape[1], corner.shape[2]
    rows = m // n
    top = jnp.zeros((m, m), jnp.float32)
    for i in range(slots):
        b_here = (bcorner[0, 0, i], bcorner[1, 0, i])
        blocks = blocks_of((turn[0:1], turn[1:2]), corner[0, i], b_here, wv[2 * i], wv[2 * i + 1])
        top = jnp.maximum(top, jnp.abs(blocks[0].astype(jnp.float32)))
        for kind in range(3):
            stage[3 * i + kind] = blocks[kind]
    peak = jnp.full((TILE, m), jnp.max(top), jnp.float32).astype(jnp.bfloat16)
    for p, k in enumerate(steps):
        first = piece_start(jnp.bitwise_xor(here[0], k), m, n, sites)
        for b in range(3 * slots):
            out[p][b * rows : (b + 1) * rows] = stage[b, pl.ds(first, rows)]
        out[p][3 * slots * rows :] = peak


def route_kernel(steps, slots, joining_in, *refs):
    n = len(steps)
    pieces, out, (held, joining, sem) = refs[:n], refs[n : 2 * n], refs[2 * n :]
    copy = pltpu.make_async_copy(joining_in, joining, sem)
    copy.start()
    here = my_place()
    size = held.shape[1]
    top = functools.reduce(jnp.maximum, [piece[slots * size :].astype(jnp.float32) for piece in pieces])
    divisor = jnp.concatenate([top] * (size // TILE), axis=0) + epsilon
    for p, k in enumerate(steps):
        d = jnp.bitwise_xor(here[0], k)
        for i in range(slots):
            piece = pieces[p][i * size : (i + 1) * size].astype(jnp.float32)
            held[d * slots + i] = (piece / divisor).astype(jnp.bfloat16)
    copy.wait()
    for p, k in enumerate(steps):
        t = jnp.bitwise_xor(here[0], k)
        for i in range(slots):
            out[p][i * size : (i + 1) * size] = held[joining[0, t * slots + i]]


def share_kernel(steps, sites, *refs):
    pieces, out, stage = refs[:sites], refs[-1 - sites : -1], refs[-1]
    here = my_place()
    _, slots, rows, _ = out[0].shape
    for p, k in enumerate(steps):
        r = lax.rem(jnp.bitwise_xor(here[0], k), sites)
        for i in range(slots):
            for c in range(2):
                at = (3 * i + 1 + c) * rows
                stage[r, c, i] = pieces[p][at : at + rows]
    for p, k in enumerate(SITE_STEPS):
        out[p][...] = stage[jnp.bitwise_xor(here[1], k)]


def sum_kernel(sites, *refs):
    near, far, summed = refs[:sites], refs[sites : 2 * sites], refs[2 * sites]
    here = my_place()
    _, slots, rows, _ = near[0].shape
    half = lax.div(here[0], sites)
    for shares, place in ((near, half), (far, 1 - half)):
        first = pl.multiple_of(place * rows, rows)
        for i in range(slots):
            for c in range(2):
                summed[c, i, pl.ds(first, rows)] = sum([share[c, i].astype(jnp.float32) for share in shares[1:]],
                                                       shares[0][c, i].astype(jnp.float32))


def join_kernel(steps, sites, *refs):
    n = len(steps)
    pieces, new_corner, new_b = refs[:n], refs[n], refs[n + 1]
    here = my_place()
    _, slots, m, _ = new_corner.shape
    rows = m // n
    for p, k in enumerate(steps):
        first = piece_start(jnp.bitwise_xor(here[0], k), m, n, sites)
        for i in range(slots):
            at = 3 * i * rows
            new_corner[0, i, pl.ds(first, rows)] = pieces[p][at : at + rows]
            for c in range(2):
                at = (3 * i + 1 + c) * rows
                new_b[c, 0, i, pl.ds(first, rows)] = pieces[p][at : at + rows]


def routed_by_tiles(turn, corner, bcorner, wv, joining, n, sites):
    _, slots, m, _ = corner.shape
    rows = m // n
    shape = lambda *dims: jax.ShapeDtypeStruct(dims, jnp.bfloat16)
    scratch = lambda *dims: [pltpu.VMEM(dims, jnp.bfloat16)]
    bind = functools.partial
    steps = start_order(n)
    pieces = [shape(3 * slots * rows + TILE, m)] * n
    kept = scratch(3 * slots, m, m)
    parts = small_call(bind(spread_kernel, steps, sites), pieces, [VMEM] * 4, kept, "spread")(
        turn, corner, bcorner, wv
    )
    parts = all_swapped(parts, steps, "blk")
    pieces = [shape(3 * slots * rows, m)] * n
    kept = scratch(n * slots, 3 * rows, m) + [pltpu.SMEM(joining.shape, jnp.int32), pltpu.SemaphoreType.DMA]
    parts = small_call(bind(route_kernel, steps, slots), pieces, [ANY] + [VMEM] * n, kept, "route")(
        joining, *parts
    )
    parts = all_swapped(parts, steps, "blk")
    halves = []
    for ours in (lambda k: k < sites, lambda k: k >= sites):
        some = [(k, part) for k, part in zip(steps, parts) if ours(k)]
        share = bind(share_kernel, [k for k, _ in some], sites)
        kept = scratch(sites, 2, slots, rows, m)
        late = [] if halves else [part for k, part in zip(steps, parts) if k in FIRST]
        specs = [VMEM] * sites + [ANY] * len(late)
        shares = small_call(share, [shape(2, slots, rows, m)] * sites, specs, kept, "share")(
            *[part for _, part in some], *late
        )
        halves += all_swapped(shares, SITE_STEPS, "site")
    pieces = [shape(1, slots, m, m), shape(2, 1, slots, m, m)]
    join = bind(join_kernel, steps, sites)
    new_corner, new_b = small_call(join, pieces, [VMEM] * n, [], "join")(*parts)
    summed = jax.ShapeDtypeStruct((2, slots, m // sites, m), jnp.float32)
    add = bind(sum_kernel, sites)
    summed = small_call(add, [summed], [VMEM] * (2 * sites), [], "sum")(*halves)[0]
    return new_corner, new_b, summed


def transposed(pieces):
    return lax.all_to_all(pieces, "blk", 0, 0, tiled=True)


def routed_by_rows(turn, corner, bcorner, wv, joining, n, sites):
    _, slots, m, _ = corner.shape
    rows = m // n
    wv = wv.reshape(slots, 2, m, m)
    ground, re, im = jax.vmap(lambda c, b, x: blocks_of((turn[0], turn[1]), c, b, x[0], x[1]))(
        corner[0], jnp.moveaxis(bcorner[:, 0], 0, 1), wv
    )
    peak = lax.pmax(jnp.max(jnp.abs(ground)).astype(jnp.float32), "blk")
    blocks = jnp.moveaxis(jnp.stack([ground, re, im], axis=1).reshape(slots, 3, n, rows, m), 2, 0)
    pieces = transposed(blocks).reshape(n * slots, 3, rows, m)
    scaled = (pieces[joining[0]].astype(jnp.float32) / (peak + epsilon)).astype(jnp.bfloat16)
    final = transposed(scaled.reshape(n, slots, 3, rows, m))
    new = jnp.transpose(final, (2, 1, 0, 3, 4)).reshape(3, slots, m, m)
    shares = jnp.moveaxis(new[1:].reshape(2, slots, sites, m // sites, m), 2, 0)
    shares = lax.all_to_all(shares, "site", 0, 0, tiled=True)
    return new[0][None], new[1:][:, None], jnp.sum(shares.astype(jnp.float32), axis=0)


def per_device(corner, bcorner, edge, bedge, proj, joining, momentum):
    m = corner.shape[2]
    n, sites = lax.axis_size("blk"), lax.axis_size("site")
    angle = momentum[0] * lax.axis_index("site").astype(jnp.float32)
    turn = jnp.broadcast_to(jnp.stack([jnp.cos(angle), jnp.sin(angle)])[:, None], (2, m))
    onward = [(i, (i + 1) % sites) for i in range(sites)]
    left_bcorner = lax.ppermute(bcorner, "site", onward)
    left_corner = lax.ppermute(corner, "site", onward)
    wv = edge_proj(edge, bedge, proj)
    routed = routed_by_tiles if m % (n * TILE) == 0 and (n, sites) == (8, len(SITE_STEPS)) else routed_by_rows
    return routed(turn, left_corner, left_bcorner, wv, joining, n, sites)


def solution(mesh):
    in_specs = (
        P("site", "blk", None, None),
        P(None, "site", "blk", None, None),
        P("site", "blk", None, None),
        P("site", "blk", None, None),
        P("site", "blk", None, None),
        P("site", None),
        P(),
    )
    out_specs = (
        P("site", "blk", None, None),
        P(None, "site", "blk", None, None),
        P(None, "blk", "site", None),
    )
    return jax.shard_map(
        per_device, mesh=mesh, in_specs=in_specs, out_specs=out_specs, check_vma=False
    )
```

profile of v0, /device:TPU:0, one launch (start us, length us, event | category | flops | bytes accessed | tf_op | source)
XLA Modules:
  0.0 53.1 jit_solution(5656263483311887564)
XLA Ops:
  0.6 0.5 collective-permute-start.1
  1.1 2.6 %collective-permute-start = (bf16[1,6,128,128]{3,2,1,0:T(8,128)(2,1)}, bf16[1,6,128,128]{3,2,1,0:T(8,128)(2,1)S(1)}, u32[]{:S(2)}, u32[]{:S(2)}) collective-permute-start(bf16[1,6,128,128]{3,2,1,0:T(8,128)(2,1)} %param.7), channel_id=1, source_target_pairs={{0,8},{8,16},{16,24},{24,0},{1,9},{9,17},{17,25},{25,1},{2,10},{10... | collective-permute-start | bytes 589832 | tf_op jit(solution)/shard_map/ppermute | solution.py:258
  4.6 5.3 %edge_proj.1.wv = bf16[12,128,128]{2,1,0:T(8,128)(2,1)S(1)} custom-call(bf16[1,6,128,2304]{3,2,1,0:T(8,128)(2,1)} %edge.1, bf16[1,6,128,2304]{3,2,1,0:T(8,128)(2,1)} %bedge.1, bf16[1,6,2304,128]{3,2,1,0:T(8,128)(2,1)} %proj.1), custom_call_target="tpu_custom_call" | custom-call | flops 905969664 | bytes 10616832 | tf_op jit(solution)/shard_map/edge_proj/pallas_call | solution.py:62
  9.9 0.1 pad_maximum_fusion
  10.0 0.9 %collective-permute-done.corner = bf16[1,6,128,128]{3,2,1,0:T(8,128)(2,1)S(1)} collective-permute-done((bf16[1,6,128,128]{3,2,1,0:T(8,128)(2,1)}, bf16[1,6,128,128]{3,2,1,0:T(8,128)(2,1)S(1)}, u32[]{:S(2)}, u32[]{:S(2)}) %collective-permute-start) | collective-permute-done | bytes 196640 | tf_op jit(solution)/shard_map/ppermute | solution.py:258
  10.9 0.0 collective-permute-done.1.bcorner
  10.9 0.1 broadcast_in_dim.2.turn
  10.9 0.5 spread.1
  11.4 4.5 %collective-permute-start.2 = (bf16[304,128]{1,0:T(8,128)(2,1)S(1)}, bf16[304,128]{1,0:T(8,128)(2,1)S(1)}, u32[]{:S(2)}, u32[]{:S(2)}) collective-permute-start(bf16[304,128]{1,0:T(8,128)(2,1)S(1)} %get-tuple-element.30), channel_id=1, source_target_pairs={{0,6},{1,7},{2,4},{3,5},{4,2},{5,3},{6,0},{7,1},{8,14},{9,15},{10,... | collective-permute-start | bytes 233480 | tf_op jit(solution)/shard_map/ppermute | solution.py:35
  15.9 1.5 %collective-permute-start.3 = (bf16[304,128]{1,0:T(8,128)(2,1)S(1)}, bf16[304,128]{1,0:T(8,128)(2,1)S(1)}, u32[]{:S(2)}, u32[]{:S(2)}) collective-permute-start(bf16[304,128]{1,0:T(8,128)(2,1)S(1)} %get-tuple-element.31), channel_id=1, source_target_pairs={{0,1},{1,0},{2,3},{3,2},{4,5},{5,4},{6,7},{7,6},{8,9},{9,8},{10,11... | collective-permute-start | bytes 233480 | tf_op jit(solution)/shard_map/ppermute | solution.py:35
  17.4 0.0 collective-permute-start.4
  17.4 1.9 %collective-permute-start.5 = (bf16[304,128]{1,0:T(8,128)(2,1)S(1)}, bf16[304,128]{1,0:T(8,128)(2,1)S(1)}, u32[]{:S(2)}, u32[]{:S(2)}) collective-permute-start(bf16[304,128]{1,0:T(8,128)(2,1)S(1)} %get-tuple-element.33), channel_id=1, source_target_pairs={{0,7},{1,6},{2,5},{3,4},{4,3},{5,2},{6,1},{7,0},{8,15},{9,14},{10,... | collective-permute-start | bytes 233480 | tf_op jit(solution)/shard_map/ppermute | solution.py:35
  19.2 1.3 %collective-permute-start.6 = (bf16[304,128]{1,0:T(8,128)(2,1)S(1)}, bf16[304,128]{1,0:T(8,128)(2,1)S(1)}, u32[]{:S(2)}, u32[]{:S(2)}) collective-permute-start(bf16[304,128]{1,0:T(8,128)(2,1)S(1)} %get-tuple-element.34), channel_id=1, source_target_pairs={{0,5},{1,4},{2,7},{3,6},{4,1},{5,0},{6,3},{7,2},{8,13},{9,12},{10,... | collective-permute-start | bytes 233480 | tf_op jit(solution)/shard_map/ppermute | solution.py:35
  20.5 0.0 collective-permute-done.2.refs_1_
  20.5 2.9 %collective-permute-start.7 = (bf16[304,128]{1,0:T(8,128)(2,1)S(1)}, bf16[304,128]{1,0:T(8,128)(2,1)S(1)}, u32[]{:S(2)}, u32[]{:S(2)}) collective-permute-start(bf16[304,128]{1,0:T(8,128)(2,1)S(1)} %get-tuple-element.35), channel_id=1, source_target_pairs={{0,2},{1,3},{2,0},{3,1},{4,6},{5,7},{6,4},{7,5},{8,10},{9,11},{10,... | collective-permute-start | bytes 233480 | tf_op jit(solution)/shard_map/ppermute | solution.py:35
  23.4 0.0 collective-permute-done.3.refs_2_
  23.4 1.3 %collective-permute-start.8 = (bf16[304,128]{1,0:T(8,128)(2,1)S(1)}, bf16[304,128]{1,0:T(8,128)(2,1)S(1)}, u32[]{:S(2)}, u32[]{:S(2)}) collective-permute-start(bf16[304,128]{1,0:T(8,128)(2,1)S(1)} %get-tuple-element.36), channel_id=1, source_target_pairs={{0,3},{1,2},{2,1},{3,0},{4,7},{5,6},{6,5},{7,4},{8,11},{9,10},{10,... | collective-permute-start | bytes 233480 | tf_op jit(solution)/shard_map/ppermute | solution.py:35
  24.7 0.9 %collective-permute-done.4.refs_3_ = bf16[304,128]{1,0:T(8,128)(2,1)S(1)} collective-permute-done((bf16[304,128]{1,0:T(8,128)(2,1)S(1)}, bf16[304,128]{1,0:T(8,128)(2,1)S(1)}, u32[]{:S(2)}, u32[]{:S(2)}) %collective-permute-start.4) | collective-permute-done | bytes 77856 | tf_op jit(solution)/shard_map/ppermute | solution.py:35
  25.6 0.0 collective-permute-done.5.refs_4_
  25.6 4.0 %collective-permute-done.6.refs_5_ = bf16[304,128]{1,0:T(8,128)(2,1)S(1)} collective-permute-done((bf16[304,128]{1,0:T(8,128)(2,1)S(1)}, bf16[304,128]{1,0:T(8,128)(2,1)S(1)}, u32[]{:S(2)}, u32[]{:S(2)}) %collective-permute-start.6) | collective-permute-done | bytes 77856 | tf_op jit(solution)/shard_map/ppermute | solution.py:35
  29.6 0.0 collective-permute-done.7.refs_6_
  29.6 0.4 collective-permute-done.8.refs_7_
  30.0 0.6 %route.1 = (bf16[288,128]{1,0:T(8,128)(2,1)S(1)}, bf16[288,128]{1,0:T(8,128)(2,1)S(1)}, bf16[288,128]{1,0:T(8,128)(2,1)S(1)}, bf16[288,128]{1,0:T(8,128)(2,1)S(1...) custom-call(s32[1,48]{1,0:T(1,128)S(1)} %copy-done, ...), custom_call_target="tpu_custom_call" | custom-call | flops 268435456 | bytes 1048576 | tf_op jit(solution)/shard_map/route/pallas_call | solution.py:205
  30.7 3.3 %collective-permute-start.9 = (bf16[288,128]{1,0:T(8,128)(2,1)S(1)}, bf16[288,128]{1,0:T(8,128)(2,1)S(1)}, u32[]{:S(2)}, u32[]{:S(2)}) collective-permute-start(bf16[288,128]{1,0:T(8,128)(2,1)S(1)} %get-tuple-element.38), channel_id=1, source_target_pairs={{0,6},{1,7},{2,4},{3,5},{4,2},{5,3},{6,0},{7,1},{8,14},{9,15},{10,... | collective-permute-start | bytes 221192 | tf_op jit(solution)/shard_map/ppermute | solution.py:35
  33.9 1.3 %collective-permute-start.10 = (bf16[288,128]{1,0:T(8,128)(2,1)S(1)}, bf16[288,128]{1,0:T(8,128)(2,1)S(1)}, u32[]{:S(2)}, u32[]{:S(2)}) collective-permute-start(bf16[288,128]{1,0:T(8,128)(2,1)S(1)} %get-tuple-element.39), channel_id=1, source_target_pairs={{0,1},{1,0},{2,3},{3,2},{4,5},{5,4},{6,7},{7,6},{8,9},{9,8},{10,11... | collective-permute-start | bytes 221192 | tf_op jit(solution)/shard_map/ppermute | solution.py:35
  35.2 0.0 collective-permute-start.11
  35.2 2.3 %collective-permute-start.12 = (bf16[288,128]{1,0:T(8,128)(2,1)S(1)}, bf16[288,128]{1,0:T(8,128)(2,1)S(1)}, u32[]{:S(2)}, u32[]{:S(2)}) collective-permute-start(bf16[288,128]{1,0:T(8,128)(2,1)S(1)} %get-tuple-element.41), channel_id=1, source_target_pairs={{0,7},{1,6},{2,5},{3,4},{4,3},{5,2},{6,1},{7,0},{8,15},{9,14},{10,... | collective-permute-start | bytes 221192 | tf_op jit(solution)/shard_map/ppermute | solution.py:35
  37.5 1.4 %collective-permute-start.14 = (bf16[288,128]{1,0:T(8,128)(2,1)S(1)}, bf16[288,128]{1,0:T(8,128)(2,1)S(1)}, u32[]{:S(2)}, u32[]{:S(2)}) collective-permute-start(bf16[288,128]{1,0:T(8,128)(2,1)S(1)} %get-tuple-element.43), channel_id=1, source_target_pairs={{0,2},{1,3},{2,0},{3,1},{4,6},{5,7},{6,4},{7,5},{8,10},{9,11},{10,... | collective-permute-start | bytes 221192 | tf_op jit(solution)/shard_map/ppermute | solution.py:35
  38.9 0.0 collective-permute-done.9.refs_1_.refs_4_.refs_0_
  38.9 1.2 %collective-permute-start.15 = (bf16[288,128]{1,0:T(8,128)(2,1)S(1)}, bf16[288,128]{1,0:T(8,128)(2,1)S(1)}, u32[]{:S(2)}, u32[]{:S(2)}) collective-permute-start(bf16[288,128]{1,0:T(8,128)(2,1)S(1)} %get-tuple-element.44), channel_id=1, source_target_pairs={{0,3},{1,2},{2,1},{3,0},{4,7},{5,6},{6,5},{7,4},{8,11},{9,10},{10,... | collective-permute-start | bytes 221192 | tf_op jit(solution)/shard_map/ppermute | solution.py:35
  40.1 0.0 collective-permute-done.10.refs_2_.refs_1_
  40.1 2.1 %collective-permute-start.13 = (bf16[288,128]{1,0:T(8,128)(2,1)S(1)}, bf16[288,128]{1,0:T(8,128)(2,1)S(1)}, u32[]{:S(2)}, u32[]{:S(2)}) collective-permute-start(bf16[288,128]{1,0:T(8,128)(2,1)S(1)} %get-tuple-element.42), channel_id=1, source_target_pairs={{0,5},{1,4},{2,7},{3,6},{4,1},{5,0},{6,3},{7,2},{8,13},{9,12},{10,... | collective-permute-start | bytes 221192 | tf_op jit(solution)/shard_map/ppermute | solution.py:35
  42.2 0.7 %collective-permute-done.11.refs_3_.refs_5_.refs_1_ = bf16[288,128]{1,0:T(8,128)(2,1)S(1)} collective-permute-done((bf16[288,128]{1,0:T(8,128)(2,1)S(1)}, bf16[288,128]{1,0:T(8,128)(2,1)S(1)}, u32[]{:S(2)}, u32[]{:S(2)}) %collective-permute-start.11) | collective-permute-done | bytes 73760 | tf_op jit(solution)/shard_map/ppermute | solution.py:35
  42.9 1.6 %collective-permute-done.15.refs_7_.refs_3_ = bf16[288,128]{1,0:T(8,128)(2,1)S(1)} collective-permute-done((bf16[288,128]{1,0:T(8,128)(2,1)S(1)}, bf16[288,128]{1,0:T(8,128)(2,1)S(1)}, u32[]{:S(2)}, u32[]{:S(2)}) %collective-permute-start.15) | collective-permute-done | bytes 73760 | tf_op jit(solution)/shard_map/ppermute | solution.py:35
  44.5 1.7 %collective-permute-start.16 = (bf16[2,6,16,128]{3,2,1,0:T(8,128)(2,1)S(1)}, bf16[2,6,16,128]{3,2,1,0:T(8,128)(2,1)S(1)}, u32[]{:S(2)}, u32[]{:S(2)}) collective-permute-start(bf16[2,6,16,128]{3,2,1,0:T(8,128)(2,1)S(1)} %get-tuple-element.48), channel_id=1, source_target_pairs={{0,16},{8,24},{16,0},{24,8},{1,17},{9,25},{17,1},{25,9},{2,18},{10... | collective-permute-start | bytes 147464 | tf_op jit(solution)/shard_map/ppermute | solution.py:35
  46.2 0.5 collective-permute-start.18
  46.7 0.0 collective-permute-done.13.refs_5_.refs_3_
  46.7 1.7 %collective-permute-start.19 = (bf16[2,6,16,128]{3,2,1,0:T(8,128)(2,1)S(1)}, bf16[2,6,16,128]{3,2,1,0:T(8,128)(2,1)S(1)}, u32[]{:S(2)}, u32[]{:S(2)}) collective-permute-start(bf16[2,6,16,128]{3,2,1,0:T(8,128)(2,1)S(1)} %get-tuple-element.52), channel_id=1, source_target_pairs={{0,16},{8,24},{16,0},{24,8},{1,17},{9,25},{17,1},{25,9},{2,18},{10... | collective-permute-start | bytes 147464 | tf_op jit(solution)/shard_map/ppermute | solution.py:35
  48.5 0.0 collective-permute-start.20
  48.5 0.2 collective-permute-done.16.refs_1_
  48.6 0.3 collective-permute-start.21
  48.9 0.9 %join.1 = (bf16[1,6,128,128]{3,2,1,0:T(8,128)(2,1)}, bf16[2,1,6,128,128]{4,3,2,1,0:T(8,128)(2,1)}) custom-call(bf16[288,128]{1,0:T(8,128)(2,1)S(1)} %get-tuple-element.37.refs_0_, bf16[288,128]{1,0:T(8,128)(2,1)S(1)} %collective-permute-done.9.refs_1_.refs_4_.refs_0_, bf16[288,128]{1,0:T(8,128)(2,1)S(1)} %collective-permute-done.10.refs_2_.refs_1_, ...), custom_call_target="tpu_custom_call" | custom-call | flops 268435456 | bytes 1048576 | tf_op jit(solution)/shard_map/join/pallas_call | solution.py:222
  49.8 0.0 collective-permute-done.17.refs_2_
  49.8 0.0 collective-permute-done.18.refs_3_
  49.8 1.0 %collective-permute-done.19.refs_5_ = bf16[2,6,16,128]{3,2,1,0:T(8,128)(2,1)S(1)} collective-permute-done((bf16[2,6,16,128]{3,2,1,0:T(8,128)(2,1)S(1)}, bf16[2,6,16,128]{3,2,1,0:T(8,128)(2,1)S(1)}, u32[]{:S(2)}, u32[]{:S(2)}) %collective-permute-start.19) | collective-permute-done | bytes 49184 | tf_op jit(solution)/shard_map/ppermute | solution.py:35
  50.9 1.5 %collective-permute-done.20.refs_6_ = bf16[2,6,16,128]{3,2,1,0:T(8,128)(2,1)S(1)} collective-permute-done((bf16[2,6,16,128]{3,2,1,0:T(8,128)(2,1)S(1)}, bf16[2,6,16,128]{3,2,1,0:T(8,128)(2,1)S(1)}, u32[]{:S(2)}, u32[]{:S(2)}) %collective-permute-start.20) | collective-permute-done | bytes 49184 | tf_op jit(solution)/shard_map/ppermute | solution.py:35
  52.4 0.0 collective-permute-done.21.refs_7_
  52.4 0.7 %sum.1 = f32[2,6,32,128]{3,2,1,0:T(8,128)} custom-call(bf16[2,6,16,128]{3,2,1,0:T(8,128)(2,1)S(1)} %get-tuple-element.47.refs_0_, bf16[2,6,16,128]{3,2,1,0:T(8,128)(2,1)S(1)} %collective-permute-done.16.refs_1_, bf16[2,6,16,128]{3,2,1,0:T(8,128)(2,1)S(1)} %collective-permute-done.17.refs_2_, bf16[2,6,16,128]{3,2,1,0:T(8,128)(2,1)S(1)} %collective-permute-done.18.refs_3_, ...), custom_call_target="tpu_custom_call" | custom-call | flops 268435456 | bytes 1048576 | tf_op jit(solution)/shard_map/sum/pallas_call | solution.py:225
  (7 shorter events, 0.1 us)
Async XLA Ops:
  0.6 10.2 %collective-permute-start.1 = (bf16[2,1,6,128,128]{4,3,2,1,0:T(8,128)(2,1)}, bf16[2,1,6,128,128]{4,3,2,1,0:T(8,128)(2,1)S(1)}, u32[]{:S(2)}, u32[]{:S(2)}) collective-permute-start(bf16[2,1,6,128,128]{4,3,2,1,0:T(8,128)(2,1)} %param.8), channel_id=1, source_target_pairs={{0,8},{8,16},{16,24},{24,0},{1,9},{9,17},{17,25},{25,1},{2,10},{10... | collective-permute-start | bytes 1179656 | tf_op jit(solution)/shard_map/ppermute | solution.py:257
  1.1 9.7 %collective-permute-start = (bf16[1,6,128,128]{3,2,1,0:T(8,128)(2,1)}, bf16[1,6,128,128]{3,2,1,0:T(8,128)(2,1)S(1)}, u32[]{:S(2)}, u32[]{:S(2)}) collective-permute-start(bf16[1,6,128,128]{3,2,1,0:T(8,128)(2,1)} %param.7), channel_id=1, source_target_pairs={{0,8},{8,16},{16,24},{24,0},{1,9},{9,17},{17,25},{25,1},{2,10},{10... | collective-permute-start | bytes 589832 | tf_op jit(solution)/shard_map/ppermute | solution.py:258
  4.6 25.5 %copy-start = (s32[1,48]{1,0:T(1,128)S(1)}, s32[1,48]{1,0:T(1,128)}, u32[]{:S(2)}) copy-start(s32[1,48]{1,0:T(1,128)} %joining_in.1) | copy-start | bytes 580
  11.4 9.1 %collective-permute-start.2 = (bf16[304,128]{1,0:T(8,128)(2,1)S(1)}, bf16[304,128]{1,0:T(8,128)(2,1)S(1)}, u32[]{:S(2)}, u32[]{:S(2)}) collective-permute-start(bf16[304,128]{1,0:T(8,128)(2,1)S(1)} %get-tuple-element.30), channel_id=1, source_target_pairs={{0,6},{1,7},{2,4},{3,5},{4,2},{5,3},{6,0},{7,1},{8,14},{9,15},{10,... | collective-permute-start | bytes 233480 | tf_op jit(solution)/shard_map/ppermute | solution.py:35
  15.9 7.6 %collective-permute-start.3 = (bf16[304,128]{1,0:T(8,128)(2,1)S(1)}, bf16[304,128]{1,0:T(8,128)(2,1)S(1)}, u32[]{:S(2)}, u32[]{:S(2)}) collective-permute-start(bf16[304,128]{1,0:T(8,128)(2,1)S(1)} %get-tuple-element.31), channel_id=1, source_target_pairs={{0,1},{1,0},{2,3},{3,2},{4,5},{5,4},{6,7},{7,6},{8,9},{9,8},{10,11... | collective-permute-start | bytes 233480 | tf_op jit(solution)/shard_map/ppermute | solution.py:35
  17.4 8.3 %collective-permute-start.4 = (bf16[304,128]{1,0:T(8,128)(2,1)S(1)}, bf16[304,128]{1,0:T(8,128)(2,1)S(1)}, u32[]{:S(2)}, u32[]{:S(2)}) collective-permute-start(bf16[304,128]{1,0:T(8,128)(2,1)S(1)} %get-tuple-element.32), channel_id=1, source_target_pairs={{0,4},{1,5},{2,6},{3,7},{4,0},{5,1},{6,2},{7,3},{8,12},{9,13},{10,... | collective-permute-start | bytes 233480 | tf_op jit(solution)/shard_map/ppermute | solution.py:35
  17.4 8.3 %collective-permute-start.5 = (bf16[304,128]{1,0:T(8,128)(2,1)S(1)}, bf16[304,128]{1,0:T(8,128)(2,1)S(1)}, u32[]{:S(2)}, u32[]{:S(2)}) collective-permute-start(bf16[304,128]{1,0:T(8,128)(2,1)S(1)} %get-tuple-element.33), channel_id=1, source_target_pairs={{0,7},{1,6},{2,5},{3,4},{4,3},{5,2},{6,1},{7,0},{8,15},{9,14},{10,... | collective-permute-start | bytes 233480 | tf_op jit(solution)/shard_map/ppermute | solution.py:35
  19.2 10.4 %collective-permute-start.6 = (bf16[304,128]{1,0:T(8,128)(2,1)S(1)}, bf16[304,128]{1,0:T(8,128)(2,1)S(1)}, u32[]{:S(2)}, u32[]{:S(2)}) collective-permute-start(bf16[304,128]{1,0:T(8,128)(2,1)S(1)} %get-tuple-element.34), channel_id=1, source_target_pairs={{0,5},{1,4},{2,7},{3,6},{4,1},{5,0},{6,3},{7,2},{8,13},{9,12},{10,... | collective-permute-start | bytes 233480 | tf_op jit(solution)/shard_map/ppermute | solution.py:35
  20.5 9.1 %collective-permute-start.7 = (bf16[304,128]{1,0:T(8,128)(2,1)S(1)}, bf16[304,128]{1,0:T(8,128)(2,1)S(1)}, u32[]{:S(2)}, u32[]{:S(2)}) collective-permute-start(bf16[304,128]{1,0:T(8,128)(2,1)S(1)} %get-tuple-element.35), channel_id=1, source_target_pairs={{0,2},{1,3},{2,0},{3,1},{4,6},{5,7},{6,4},{7,5},{8,10},{9,11},{10,... | collective-permute-start | bytes 233480 | tf_op jit(solution)/shard_map/ppermute | solution.py:35
  23.4 6.6 %collective-permute-start.8 = (bf16[304,128]{1,0:T(8,128)(2,1)S(1)}, bf16[304,128]{1,0:T(8,128)(2,1)S(1)}, u32[]{:S(2)}, u32[]{:S(2)}) collective-permute-start(bf16[304,128]{1,0:T(8,128)(2,1)S(1)} %get-tuple-element.36), channel_id=1, source_target_pairs={{0,3},{1,2},{2,1},{3,0},{4,7},{5,6},{6,5},{7,4},{8,11},{9,10},{10,... | collective-permute-start | bytes 233480 | tf_op jit(solution)/shard_map/ppermute | solution.py:35
  30.7 8.2 %collective-permute-start.9 = (bf16[288,128]{1,0:T(8,128)(2,1)S(1)}, bf16[288,128]{1,0:T(8,128)(2,1)S(1)}, u32[]{:S(2)}, u32[]{:S(2)}) collective-permute-start(bf16[288,128]{1,0:T(8,128)(2,1)S(1)} %get-tuple-element.38), channel_id=1, source_target_pairs={{0,6},{1,7},{2,4},{3,5},{4,2},{5,3},{6,0},{7,1},{8,14},{9,15},{10,... | collective-permute-start | bytes 221192 | tf_op jit(solution)/shard_map/ppermute | solution.py:35
  33.9 6.2 %collective-permute-start.10 = (bf16[288,128]{1,0:T(8,128)(2,1)S(1)}, bf16[288,128]{1,0:T(8,128)(2,1)S(1)}, u32[]{:S(2)}, u32[]{:S(2)}) collective-permute-start(bf16[288,128]{1,0:T(8,128)(2,1)S(1)} %get-tuple-element.39), channel_id=1, source_target_pairs={{0,1},{1,0},{2,3},{3,2},{4,5},{5,4},{6,7},{7,6},{8,9},{9,8},{10,11... | collective-permute-start | bytes 221192 | tf_op jit(solution)/shard_map/ppermute | solution.py:35
  35.2 7.7 %collective-permute-start.11 = (bf16[288,128]{1,0:T(8,128)(2,1)S(1)}, bf16[288,128]{1,0:T(8,128)(2,1)S(1)}, u32[]{:S(2)}, u32[]{:S(2)}) collective-permute-start(bf16[288,128]{1,0:T(8,128)(2,1)S(1)} %get-tuple-element.40), channel_id=1, source_target_pairs={{0,4},{1,5},{2,6},{3,7},{4,0},{5,1},{6,2},{7,3},{8,12},{9,13},{10,... | collective-permute-start | bytes 221192 | tf_op jit(solution)/shard_map/ppermute | solution.py:35
  35.2 7.7 %collective-permute-start.12 = (bf16[288,128]{1,0:T(8,128)(2,1)S(1)}, bf16[288,128]{1,0:T(8,128)(2,1)S(1)}, u32[]{:S(2)}, u32[]{:S(2)}) collective-permute-start(bf16[288,128]{1,0:T(8,128)(2,1)S(1)} %get-tuple-element.41), channel_id=1, source_target_pairs={{0,7},{1,6},{2,5},{3,4},{4,3},{5,2},{6,1},{7,0},{8,15},{9,14},{10,... | collective-permute-start | bytes 221192 | tf_op jit(solution)/shard_map/ppermute | solution.py:35
  37.5 5.4 %collective-permute-start.14 = (bf16[288,128]{1,0:T(8,128)(2,1)S(1)}, bf16[288,128]{1,0:T(8,128)(2,1)S(1)}, u32[]{:S(2)}, u32[]{:S(2)}) collective-permute-start(bf16[288,128]{1,0:T(8,128)(2,1)S(1)} %get-tuple-element.43), channel_id=1, source_target_pairs={{0,2},{1,3},{2,0},{3,1},{4,6},{5,7},{6,4},{7,5},{8,10},{9,11},{10,... | collective-permute-start | bytes 221192 | tf_op jit(solution)/shard_map/ppermute | solution.py:35
  38.9 5.6 %collective-permute-start.15 = (bf16[288,128]{1,0:T(8,128)(2,1)S(1)}, bf16[288,128]{1,0:T(8,128)(2,1)S(1)}, u32[]{:S(2)}, u32[]{:S(2)}) collective-permute-start(bf16[288,128]{1,0:T(8,128)(2,1)S(1)} %get-tuple-element.44), channel_id=1, source_target_pairs={{0,3},{1,2},{2,1},{3,0},{4,7},{5,6},{6,5},{7,4},{8,11},{9,10},{10,... | collective-permute-start | bytes 221192 | tf_op jit(solution)/shard_map/ppermute | solution.py:35
  40.1 6.6 %collective-permute-start.13 = (bf16[288,128]{1,0:T(8,128)(2,1)S(1)}, bf16[288,128]{1,0:T(8,128)(2,1)S(1)}, u32[]{:S(2)}, u32[]{:S(2)}) collective-permute-start(bf16[288,128]{1,0:T(8,128)(2,1)S(1)} %get-tuple-element.42), channel_id=1, source_target_pairs={{0,5},{1,4},{2,7},{3,6},{4,1},{5,0},{6,3},{7,2},{8,13},{9,12},{10,... | collective-permute-start | bytes 221192 | tf_op jit(solution)/shard_map/ppermute | solution.py:35
  44.5 4.2 %collective-permute-start.16 = (bf16[2,6,16,128]{3,2,1,0:T(8,128)(2,1)S(1)}, bf16[2,6,16,128]{3,2,1,0:T(8,128)(2,1)S(1)}, u32[]{:S(2)}, u32[]{:S(2)}) collective-permute-start(bf16[2,6,16,128]{3,2,1,0:T(8,128)(2,1)S(1)} %get-tuple-element.48), channel_id=1, source_target_pairs={{0,16},{8,24},{16,0},{24,8},{1,17},{9,25},{17,1},{25,9},{2,18},{10... | collective-permute-start | bytes 147464 | tf_op jit(solution)/shard_map/ppermute | solution.py:35
  46.2 3.6 %collective-permute-start.17 = (bf16[2,6,16,128]{3,2,1,0:T(8,128)(2,1)S(1)}, bf16[2,6,16,128]{3,2,1,0:T(8,128)(2,1)S(1)}, u32[]{:S(2)}, u32[]{:S(2)}) collective-permute-start(bf16[2,6,16,128]{3,2,1,0:T(8,128)(2,1)S(1)} %get-tuple-element.49), channel_id=1, source_target_pairs={{0,24},{8,16},{16,8},{24,0},{1,25},{9,17},{17,9},{25,1},{2,26},{10... | collective-permute-start | bytes 147464 | tf_op jit(solution)/shard_map/ppermute | solution.py:35
  46.2 3.6 %collective-permute-start.18 = (bf16[2,6,16,128]{3,2,1,0:T(8,128)(2,1)S(1)}, bf16[2,6,16,128]{3,2,1,0:T(8,128)(2,1)S(1)}, u32[]{:S(2)}, u32[]{:S(2)}) collective-permute-start(bf16[2,6,16,128]{3,2,1,0:T(8,128)(2,1)S(1)} %get-tuple-element.50), channel_id=1, source_target_pairs={{0,8},{8,0},{16,24},{24,16},{1,9},{9,1},{17,25},{25,17},{2,10},{10... | collective-permute-start | bytes 147464 | tf_op jit(solution)/shard_map/ppermute | solution.py:35
  46.7 4.2 %collective-permute-start.19 = (bf16[2,6,16,128]{3,2,1,0:T(8,128)(2,1)S(1)}, bf16[2,6,16,128]{3,2,1,0:T(8,128)(2,1)S(1)}, u32[]{:S(2)}, u32[]{:S(2)}) collective-permute-start(bf16[2,6,16,128]{3,2,1,0:T(8,128)(2,1)S(1)} %get-tuple-element.52), channel_id=1, source_target_pairs={{0,16},{8,24},{16,0},{24,8},{1,17},{9,25},{17,1},{25,9},{2,18},{10... | collective-permute-start | bytes 147464 | tf_op jit(solution)/shard_map/ppermute | solution.py:35
  48.5 3.9 %collective-permute-start.20 = (bf16[2,6,16,128]{3,2,1,0:T(8,128)(2,1)S(1)}, bf16[2,6,16,128]{3,2,1,0:T(8,128)(2,1)S(1)}, u32[]{:S(2)}, u32[]{:S(2)}) collective-permute-start(bf16[2,6,16,128]{3,2,1,0:T(8,128)(2,1)S(1)} %get-tuple-element.53), channel_id=1, source_target_pairs={{0,24},{8,16},{16,8},{24,0},{1,25},{9,17},{17,9},{25,1},{2,26},{10... | collective-permute-start | bytes 147464 | tf_op jit(solution)/shard_map/ppermute | solution.py:35
  48.6 3.8 %collective-permute-start.21 = (bf16[2,6,16,128]{3,2,1,0:T(8,128)(2,1)S(1)}, bf16[2,6,16,128]{3,2,1,0:T(8,128)(2,1)S(1)}, u32[]{:S(2)}, u32[]{:S(2)}) collective-permute-start(bf16[2,6,16,128]{3,2,1,0:T(8,128)(2,1)S(1)} %get-tuple-element.54), channel_id=1, source_target_pairs={{0,8},{8,0},{16,24},{24,16},{1,9},{9,1},{17,25},{25,17},{2,10},{10... | collective-permute-start | bytes 147464 | tf_op jit(solution)/shard_map/ppermute | solution.py:35
where the time goes:
time: 53.3 us; the launch traced here: 53.1 us
  starting transfers between devices  32.2 us (60%)
  waiting for transfers between devices  11.2 us (21%)
  Pallas kernels  8.07 us (15%)
  between operations  1.51 us (3%)
    ppermute x20, starting transfers between devices, all_swapped(): lax.ppermute(part, axis, [(i, i ^ k) for i in range(n)])  29 us
    ppermute x20, waiting for transfers between devices, all_swapped(): lax.ppermute(part, axis, [(i, i ^ k) for i in range(n)])  10.3 us
    pallas_call x1, Pallas kernels, edge_proj(): pl.pallas_call(edge_proj_kernel, out_shape=jax.ShapeDtypeStruct((2 * slot...  5.28 us
    ppermute x1, starting transfers between devices, per_device(): left_corner = lax.ppermute(corner, 'site', onward)  2.63 us
  transfers between devices with their start and end apart: 22, of which 9 were waited for; matrix products, arithmetic and copies ran while one was open for 0% of the time, Pallas kernels for 12%

commit v1 on v0

--- a/solution.py
+++ b/solution.py
@@ -123,12 +123,22 @@
         out[p][3 * slots * rows :] = peak
 
 
-def route_kernel(steps, slots, joining_in, *refs):
+def route_kernel(steps, slots, joining, *refs):
     n = len(steps)
-    pieces, out, (held, joining, sem) = refs[:n], refs[n : 2 * n], refs[2 * n :]
-    copy = pltpu.make_async_copy(joining_in, joining, sem)
-    copy.start()
-    here = my_place()
+    pieces, out, held = refs[:n], refs[n : 2 * n], refs[2 * n]
+    here = my_place()
+    bits = (n * slots - 1).bit_length()
+    row = joining[...]
+    lane = lax.broadcasted_iota(jnp.int32, row.shape, 1)
+
+    def sources(first):
+        at = lane - first
+        inside = jnp.logical_and(at >= 0, at < 3)
+        packed = jnp.sum(jnp.where(inside, lax.shift_left(row, bits * jnp.where(inside, at, 0)), 0))
+        return [jnp.bitwise_and(lax.shift_right_logical(packed, bits * i), (1 << bits) - 1) for i in range(3)]
+
+    owners = [jnp.bitwise_xor(here[0], k) for k in steps]
+    wanted = [[q for i in range(0, slots, 3) for q in sources(t * slots + i)] for t in owners]
     size = held.shape[1]
     top = functools.reduce(jnp.maximum, [piece[slots * size :].astype(jnp.float32) for piece in pieces])
     divisor = jnp.concatenate([top] * (size // TILE), axis=0) + epsilon
@@ -137,11 +147,9 @@
         for i in range(slots):
             piece = pieces[p][i * size : (i + 1) * size].astype(jnp.float32)
             held[d * slots + i] = (piece / divisor).astype(jnp.bfloat16)
-    copy.wait()
-    for p, k in enumerate(steps):
-        t = jnp.bitwise_xor(here[0], k)
-        for i in range(slots):
-            out[p][i * size : (i + 1) * size] = held[joining[0, t * slots + i]]
+    for p in range(n):
+        for i in range(slots):
+            out[p][i * size : (i + 1) * size] = held[wanted[p][i]]
 
 
 def share_kernel(steps, sites, *refs):
@@ -201,8 +209,8 @@
     )
     parts = all_swapped(parts, steps, "blk")
     pieces = [shape(3 * slots * rows, m)] * n
-    kept = scratch(n * slots, 3 * rows, m) + [pltpu.SMEM(joining.shape, jnp.int32), pltpu.SemaphoreType.DMA]
-    parts = small_call(bind(route_kernel, steps, slots), pieces, [ANY] + [VMEM] * n, kept, "route")(
+    kept = scratch(n * slots, 3 * rows, m)
+    parts = small_call(bind(route_kernel, steps, slots), pieces, [VMEM] * (n + 1), kept, "route")(
         joining, *parts
     )
     parts = all_swapped(parts, steps, "blk")

time: 53.3 us -> 53 us (level)
  no operation moved by 1% of the time
where the time goes in v1:
time: 53 us; the launch traced here: 52.8 us
  starting transfers between devices  32.2 us (61%)
  waiting for transfers between devices  11.2 us (21%)
  Pallas kernels  7.76 us (15%)
  between operations  1.5 us (3%)
    ppermute x20, starting transfers between devices, all_swapped(): lax.ppermute(part, axis, [(i, i ^ k) for i in range(n)])  29 us
    ppermute x20, waiting for transfers between devices, all_swapped(): lax.ppermute(part, axis, [(i, i ^ k) for i in range(n)])  10.3 us
    pallas_call x1, Pallas kernels, edge_proj(): pl.pallas_call(edge_proj_kernel, out_shape=jax.ShapeDtypeStruct((2 * slot...  5.28 us
    ppermute x1, starting transfers between devices, per_device(): left_corner = lax.ppermute(corner, 'site', onward)  2.63 us
  transfers between devices with their start and end apart: 22, of which 9 were waited for; matrix products, arithmetic and copies ran while one was open for 0% of the time, Pallas kernels for 12%

profile of v1, /device:TPU:0, one launch (start us, length us, event | category | flops | bytes accessed | tf_op | source)
XLA Modules:
  0.0 52.8 jit_solution(422277102137747697)
XLA Ops:
  0.6 0.5 collective-permute-start.1
  1.1 2.6 %collective-permute-start = (bf16[1,6,128,128]{3,2,1,0:T(8,128)(2,1)}, bf16[1,6,128,128]{3,2,1,0:T(8,128)(2,1)S(1)}, u32[]{:S(2)}, u32[]{:S(2)}) collective-permute-start(bf16[1,6,128,128]{3,2,1,0:T(8,128)(2,1)} %param.7), channel_id=1, source_target_pairs={{0,8},{8,16},{16,24},{24,0},{1,9},{9,17},{17,25},{25,1},{2,10},{10... | collective-permute-start | bytes 589832 | tf_op jit(solution)/shard_map/ppermute | solution.py:266
  4.6 5.3 %edge_proj.1.wv = bf16[12,128,128]{2,1,0:T(8,128)(2,1)S(1)} custom-call(bf16[1,6,128,2304]{3,2,1,0:T(8,128)(2,1)} %edge.1, bf16[1,6,128,2304]{3,2,1,0:T(8,128)(2,1)} %bedge.1, bf16[1,6,2304,128]{3,2,1,0:T(8,128)(2,1)} %proj.1), custom_call_target="tpu_custom_call" | custom-call | flops 905969664 | bytes 10616832 | tf_op jit(solution)/shard_map/edge_proj/pallas_call | solution.py:62
  9.9 0.1 pad_maximum_fusion
  10.0 0.9 %collective-permute-done.corner = bf16[1,6,128,128]{3,2,1,0:T(8,128)(2,1)S(1)} collective-permute-done((bf16[1,6,128,128]{3,2,1,0:T(8,128)(2,1)}, bf16[1,6,128,128]{3,2,1,0:T(8,128)(2,1)S(1)}, u32[]{:S(2)}, u32[]{:S(2)}) %collective-permute-start) | collective-permute-done | bytes 196640 | tf_op jit(solution)/shard_map/ppermute | solution.py:266
  10.9 0.0 collective-permute-done.1.bcorner
  10.9 0.1 broadcast_in_dim.2.turn
  10.9 0.5 spread.1
  11.4 4.5 %collective-permute-start.2 = (bf16[304,128]{1,0:T(8,128)(2,1)S(1)}, bf16[304,128]{1,0:T(8,128)(2,1)S(1)}, u32[]{:S(2)}, u32[]{:S(2)}) collective-permute-start(bf16[304,128]{1,0:T(8,128)(2,1)S(1)} %get-tuple-element.30), channel_id=1, source_target_pairs={{0,6},{1,7},{2,4},{3,5},{4,2},{5,3},{6,0},{7,1},{8,14},{9,15},{10,... | collective-permute-start | bytes 233480 | tf_op jit(solution)/shard_map/ppermute | solution.py:35
  15.9 1.5 %collective-permute-start.3 = (bf16[304,128]{1,0:T(8,128)(2,1)S(1)}, bf16[304,128]{1,0:T(8,128)(2,1)S(1)}, u32[]{:S(2)}, u32[]{:S(2)}) collective-permute-start(bf16[304,128]{1,0:T(8,128)(2,1)S(1)} %get-tuple-element.31), channel_id=1, source_target_pairs={{0,1},{1,0},{2,3},{3,2},{4,5},{5,4},{6,7},{7,6},{8,9},{9,8},{10,11... | collective-permute-start | bytes 233480 | tf_op jit(solution)/shard_map/ppermute | solution.py:35
  17.4 0.0 collective-permute-start.4
  17.4 1.9 %collective-permute-start.5 = (bf16[304,128]{1,0:T(8,128)(2,1)S(1)}, bf16[304,128]{1,0:T(8,128)(2,1)S(1)}, u32[]{:S(2)}, u32[]{:S(2)}) collective-permute-start(bf16[304,128]{1,0:T(8,128)(2,1)S(1)} %get-tuple-element.33), channel_id=1, source_target_pairs={{0,7},{1,6},{2,5},{3,4},{4,3},{5,2},{6,1},{7,0},{8,15},{9,14},{10,... | collective-permute-start | bytes 233480 | tf_op jit(solution)/shard_map/ppermute | solution.py:35
  19.2 1.3 %collective-permute-start.6 = (bf16[304,128]{1,0:T(8,128)(2,1)S(1)}, bf16[304,128]{1,0:T(8,128)(2,1)S(1)}, u32[]{:S(2)}, u32[]{:S(2)}) collective-permute-start(bf16[304,128]{1,0:T(8,128)(2,1)S(1)} %get-tuple-element.34), channel_id=1, source_target_pairs={{0,5},{1,4},{2,7},{3,6},{4,1},{5,0},{6,3},{7,2},{8,13},{9,12},{10,... | collective-permute-start | bytes 233480 | tf_op jit(solution)/shard_map/ppermute | solution.py:35
  20.5 0.0 collective-permute-done.2.refs_1_
  20.5 2.9 %collective-permute-start.7 = (bf16[304,128]{1,0:T(8,128)(2,1)S(1)}, bf16[304,128]{1,0:T(8,128)(2,1)S(1)}, u32[]{:S(2)}, u32[]{:S(2)}) collective-permute-start(bf16[304,128]{1,0:T(8,128)(2,1)S(1)} %get-tuple-element.35), channel_id=1, source_target_pairs={{0,2},{1,3},{2,0},{3,1},{4,6},{5,7},{6,4},{7,5},{8,10},{9,11},{10,... | collective-permute-start | bytes 233480 | tf_op jit(solution)/shard_map/ppermute | solution.py:35
  23.4 0.0 collective-permute-done.3.refs_2_
  23.4 1.3 %collective-permute-start.8 = (bf16[304,128]{1,0:T(8,128)(2,1)S(1)}, bf16[304,128]{1,0:T(8,128)(2,1)S(1)}, u32[]{:S(2)}, u32[]{:S(2)}) collective-permute-start(bf16[304,128]{1,0:T(8,128)(2,1)S(1)} %get-tuple-element.36), channel_id=1, source_target_pairs={{0,3},{1,2},{2,1},{3,0},{4,7},{5,6},{6,5},{7,4},{8,11},{9,10},{10,... | collective-permute-start | bytes 233480 | tf_op jit(solution)/shard_map/ppermute | solution.py:35
  24.7 0.9 %collective-permute-done.4.refs_3_ = bf16[304,128]{1,0:T(8,128)(2,1)S(1)} collective-permute-done((bf16[304,128]{1,0:T(8,128)(2,1)S(1)}, bf16[304,128]{1,0:T(8,128)(2,1)S(1)}, u32[]{:S(2)}, u32[]{:S(2)}) %collective-permute-start.4) | collective-permute-done | bytes 77856 | tf_op jit(solution)/shard_map/ppermute | solution.py:35
  25.6 0.0 collective-permute-done.5.refs_4_
  25.6 4.0 %collective-permute-done.6.refs_5_ = bf16[304,128]{1,0:T(8,128)(2,1)S(1)} collective-permute-done((bf16[304,128]{1,0:T(8,128)(2,1)S(1)}, bf16[304,128]{1,0:T(8,128)(2,1)S(1)}, u32[]{:S(2)}, u32[]{:S(2)}) %collective-permute-start.6) | collective-permute-done | bytes 77856 | tf_op jit(solution)/shard_map/ppermute | solution.py:35
  29.6 0.0 collective-permute-done.7.refs_6_
  29.6 0.4 collective-permute-done.8.refs_7_
  30.0 0.3 route.1
  30.4 3.3 %collective-permute-start.9 = (bf16[288,128]{1,0:T(8,128)(2,1)S(1)}, bf16[288,128]{1,0:T(8,128)(2,1)S(1)}, u32[]{:S(2)}, u32[]{:S(2)}) collective-permute-start(bf16[288,128]{1,0:T(8,128)(2,1)S(1)} %get-tuple-element.38), channel_id=1, source_target_pairs={{0,6},{1,7},{2,4},{3,5},{4,2},{5,3},{6,0},{7,1},{8,14},{9,15},{10,... | collective-permute-start | bytes 221192 | tf_op jit(solution)/shard_map/ppermute | solution.py:35
  33.6 1.2 %collective-permute-start.10 = (bf16[288,128]{1,0:T(8,128)(2,1)S(1)}, bf16[288,128]{1,0:T(8,128)(2,1)S(1)}, u32[]{:S(2)}, u32[]{:S(2)}) collective-permute-start(bf16[288,128]{1,0:T(8,128)(2,1)S(1)} %get-tuple-element.39), channel_id=1, source_target_pairs={{0,1},{1,0},{2,3},{3,2},{4,5},{5,4},{6,7},{7,6},{8,9},{9,8},{10,11... | collective-permute-start | bytes 221192 | tf_op jit(solution)/shard_map/ppermute | solution.py:35
  34.9 0.0 collective-permute-start.11
  34.9 2.3 %collective-permute-start.12 = (bf16[288,128]{1,0:T(8,128)(2,1)S(1)}, bf16[288,128]{1,0:T(8,128)(2,1)S(1)}, u32[]{:S(2)}, u32[]{:S(2)}) collective-permute-start(bf16[288,128]{1,0:T(8,128)(2,1)S(1)} %get-tuple-element.41), channel_id=1, source_target_pairs={{0,7},{1,6},{2,5},{3,4},{4,3},{5,2},{6,1},{7,0},{8,15},{9,14},{10,... | collective-permute-start | bytes 221192 | tf_op jit(solution)/shard_map/ppermute | solution.py:35
  37.1 1.4 %collective-permute-start.14 = (bf16[288,128]{1,0:T(8,128)(2,1)S(1)}, bf16[288,128]{1,0:T(8,128)(2,1)S(1)}, u32[]{:S(2)}, u32[]{:S(2)}) collective-permute-start(bf16[288,128]{1,0:T(8,128)(2,1)S(1)} %get-tuple-element.43), channel_id=1, source_target_pairs={{0,2},{1,3},{2,0},{3,1},{4,6},{5,7},{6,4},{7,5},{8,10},{9,11},{10,... | collective-permute-start | bytes 221192 | tf_op jit(solution)/shard_map/ppermute | solution.py:35
  38.6 0.0 collective-permute-done.9.refs_1_.refs_4_.refs_0_
  38.6 1.2 %collective-permute-start.15 = (bf16[288,128]{1,0:T(8,128)(2,1)S(1)}, bf16[288,128]{1,0:T(8,128)(2,1)S(1)}, u32[]{:S(2)}, u32[]{:S(2)}) collective-permute-start(bf16[288,128]{1,0:T(8,128)(2,1)S(1)} %get-tuple-element.44), channel_id=1, source_target_pairs={{0,3},{1,2},{2,1},{3,0},{4,7},{5,6},{6,5},{7,4},{8,11},{9,10},{10,... | collective-permute-start | bytes 221192 | tf_op jit(solution)/shard_map/ppermute | solution.py:35
  39.8 0.0 collective-permute-done.10.refs_2_.refs_1_
  39.8 2.1 %collective-permute-start.13 = (bf16[288,128]{1,0:T(8,128)(2,1)S(1)}, bf16[288,128]{1,0:T(8,128)(2,1)S(1)}, u32[]{:S(2)}, u32[]{:S(2)}) collective-permute-start(bf16[288,128]{1,0:T(8,128)(2,1)S(1)} %get-tuple-element.42), channel_id=1, source_target_pairs={{0,5},{1,4},{2,7},{3,6},{4,1},{5,0},{6,3},{7,2},{8,13},{9,12},{10,... | collective-permute-start | bytes 221192 | tf_op jit(solution)/shard_map/ppermute | solution.py:35
  41.8 0.7 %collective-permute-done.11.refs_3_.refs_5_.refs_1_ = bf16[288,128]{1,0:T(8,128)(2,1)S(1)} collective-permute-done((bf16[288,128]{1,0:T(8,128)(2,1)S(1)}, bf16[288,128]{1,0:T(8,128)(2,1)S(1)}, u32[]{:S(2)}, u32[]{:S(2)}) %collective-permute-start.11) | collective-permute-done | bytes 73760 | tf_op jit(solution)/shard_map/ppermute | solution.py:35
  42.5 0.0 collective-permute-done.12.refs_4_.refs_6_.refs_2_
  42.5 0.0 collective-permute-done.14.refs_6_.refs_2_
  42.5 1.6 %collective-permute-done.15.refs_7_.refs_3_ = bf16[288,128]{1,0:T(8,128)(2,1)S(1)} collective-permute-done((bf16[288,128]{1,0:T(8,128)(2,1)S(1)}, bf16[288,128]{1,0:T(8,128)(2,1)S(1)}, u32[]{:S(2)}, u32[]{:S(2)}) %collective-permute-start.15) | collective-permute-done | bytes 73760 | tf_op jit(solution)/shard_map/ppermute | solution.py:35
  44.2 1.7 %collective-permute-start.16 = (bf16[2,6,16,128]{3,2,1,0:T(8,128)(2,1)S(1)}, bf16[2,6,16,128]{3,2,1,0:T(8,128)(2,1)S(1)}, u32[]{:S(2)}, u32[]{:S(2)}) collective-permute-start(bf16[2,6,16,128]{3,2,1,0:T(8,128)(2,1)S(1)} %get-tuple-element.48), channel_id=1, source_target_pairs={{0,16},{8,24},{16,0},{24,8},{1,17},{9,25},{17,1},{25,9},{2,18},{10... | collective-permute-start | bytes 147464 | tf_op jit(solution)/shard_map/ppermute | solution.py:35
  45.9 0.5 collective-permute-start.18
  46.4 1.7 %collective-permute-start.19 = (bf16[2,6,16,128]{3,2,1,0:T(8,128)(2,1)S(1)}, bf16[2,6,16,128]{3,2,1,0:T(8,128)(2,1)S(1)}, u32[]{:S(2)}, u32[]{:S(2)}) collective-permute-start(bf16[2,6,16,128]{3,2,1,0:T(8,128)(2,1)S(1)} %get-tuple-element.52), channel_id=1, source_target_pairs={{0,16},{8,24},{16,0},{24,8},{1,17},{9,25},{17,1},{25,9},{2,18},{10... | collective-permute-start | bytes 147464 | tf_op jit(solution)/shard_map/ppermute | solution.py:35
  48.1 0.0 collective-permute-start.20
  48.1 0.2 collective-permute-done.16.refs_1_
  48.3 0.3 collective-permute-start.21
  48.6 0.9 %join.1 = (bf16[1,6,128,128]{3,2,1,0:T(8,128)(2,1)}, bf16[2,1,6,128,128]{4,3,2,1,0:T(8,128)(2,1)}) custom-call(bf16[288,128]{1,0:T(8,128)(2,1)S(1)} %get-tuple-element.37.refs_0_, bf16[288,128]{1,0:T(8,128)(2,1)S(1)} %collective-permute-done.9.refs_1_.refs_4_.refs_0_, bf16[288,128]{1,0:T(8,128)(2,1)S(1)} %collective-permute-done.10.refs_2_.refs_1_, ...), custom_call_target="tpu_custom_call" | custom-call | flops 268435456 | bytes 1048576 | tf_op jit(solution)/shard_map/join/pallas_call | solution.py:230
  49.5 0.0 collective-permute-done.17.refs_2_
  49.5 0.0 collective-permute-done.18.refs_3_
  49.5 1.0 %collective-permute-done.19.refs_5_ = bf16[2,6,16,128]{3,2,1,0:T(8,128)(2,1)S(1)} collective-permute-done((bf16[2,6,16,128]{3,2,1,0:T(8,128)(2,1)S(1)}, bf16[2,6,16,128]{3,2,1,0:T(8,128)(2,1)S(1)}, u32[]{:S(2)}, u32[]{:S(2)}) %collective-permute-start.19) | collective-permute-done | bytes 49184 | tf_op jit(solution)/shard_map/ppermute | solution.py:35
  50.6 1.5 %collective-permute-done.20.refs_6_ = bf16[2,6,16,128]{3,2,1,0:T(8,128)(2,1)S(1)} collective-permute-done((bf16[2,6,16,128]{3,2,1,0:T(8,128)(2,1)S(1)}, bf16[2,6,16,128]{3,2,1,0:T(8,128)(2,1)S(1)}, u32[]{:S(2)}, u32[]{:S(2)}) %collective-permute-start.20) | collective-permute-done | bytes 49184 | tf_op jit(solution)/shard_map/ppermute | solution.py:35
  52.1 0.7 %sum.1 = f32[2,6,32,128]{3,2,1,0:T(8,128)} custom-call(bf16[2,6,16,128]{3,2,1,0:T(8,128)(2,1)S(1)} %get-tuple-element.47.refs_0_, bf16[2,6,16,128]{3,2,1,0:T(8,128)(2,1)S(1)} %collective-permute-done.16.refs_1_, bf16[2,6,16,128]{3,2,1,0:T(8,128)(2,1)S(1)} %collective-permute-done.17.refs_2_, bf16[2,6,16,128]{3,2,1,0:T(8,128)(2,1)S(1)} %collective-permute-done.18.refs_3_, ...), custom_call_target="tpu_custom_call" | custom-call | flops 268435456 | bytes 1048576 | tf_op jit(solution)/shard_map/sum/pallas_call | solution.py:233
  (7 shorter events, 0.1 us)
Async XLA Ops:
  0.6 10.2 %collective-permute-start.1 = (bf16[2,1,6,128,128]{4,3,2,1,0:T(8,128)(2,1)}, bf16[2,1,6,128,128]{4,3,2,1,0:T(8,128)(2,1)S(1)}, u32[]{:S(2)}, u32[]{:S(2)}) collective-permute-start(bf16[2,1,6,128,128]{4,3,2,1,0:T(8,128)(2,1)} %param.8), channel_id=1, source_target_pairs={{0,8},{8,16},{16,24},{24,0},{1,9},{9,17},{17,25},{25,1},{2,10},{10... | collective-permute-start | bytes 1179656 | tf_op jit(solution)/shard_map/ppermute | solution.py:265
  1.1 9.7 %collective-permute-start = (bf16[1,6,128,128]{3,2,1,0:T(8,128)(2,1)}, bf16[1,6,128,128]{3,2,1,0:T(8,128)(2,1)S(1)}, u32[]{:S(2)}, u32[]{:S(2)}) collective-permute-start(bf16[1,6,128,128]{3,2,1,0:T(8,128)(2,1)} %param.7), channel_id=1, source_target_pairs={{0,8},{8,16},{16,24},{24,0},{1,9},{9,17},{17,25},{25,1},{2,10},{10... | collective-permute-start | bytes 589832 | tf_op jit(solution)/shard_map/ppermute | solution.py:266
  4.6 25.5 %copy-start = (s32[1,48]{1,0:T(1,128)S(1)}, s32[1,48]{1,0:T(1,128)}, u32[]{:S(2)}) copy-start(s32[1,48]{1,0:T(1,128)} %joining.1) | copy-start | bytes 580
  11.4 9.1 %collective-permute-start.2 = (bf16[304,128]{1,0:T(8,128)(2,1)S(1)}, bf16[304,128]{1,0:T(8,128)(2,1)S(1)}, u32[]{:S(2)}, u32[]{:S(2)}) collective-permute-start(bf16[304,128]{1,0:T(8,128)(2,1)S(1)} %get-tuple-element.30), channel_id=1, source_target_pairs={{0,6},{1,7},{2,4},{3,5},{4,2},{5,3},{6,0},{7,1},{8,14},{9,15},{10,... | collective-permute-start | bytes 233480 | tf_op jit(solution)/shard_map/ppermute | solution.py:35
  15.9 7.6 %collective-permute-start.3 = (bf16[304,128]{1,0:T(8,128)(2,1)S(1)}, bf16[304,128]{1,0:T(8,128)(2,1)S(1)}, u32[]{:S(2)}, u32[]{:S(2)}) collective-permute-start(bf16[304,128]{1,0:T(8,128)(2,1)S(1)} %get-tuple-element.31), channel_id=1, source_target_pairs={{0,1},{1,0},{2,3},{3,2},{4,5},{5,4},{6,7},{7,6},{8,9},{9,8},{10,11... | collective-permute-start | bytes 233480 | tf_op jit(solution)/shard_map/ppermute | solution.py:35
  17.4 8.3 %collective-permute-start.4 = (bf16[304,128]{1,0:T(8,128)(2,1)S(1)}, bf16[304,128]{1,0:T(8,128)(2,1)S(1)}, u32[]{:S(2)}, u32[]{:S(2)}) collective-permute-start(bf16[304,128]{1,0:T(8,128)(2,1)S(1)} %get-tuple-element.32), channel_id=1, source_target_pairs={{0,4},{1,5},{2,6},{3,7},{4,0},{5,1},{6,2},{7,3},{8,12},{9,13},{10,... | collective-permute-start | bytes 233480 | tf_op jit(solution)/shard_map/ppermute | solution.py:35
  17.4 8.3 %collective-permute-start.5 = (bf16[304,128]{1,0:T(8,128)(2,1)S(1)}, bf16[304,128]{1,0:T(8,128)(2,1)S(1)}, u32[]{:S(2)}, u32[]{:S(2)}) collective-permute-start(bf16[304,128]{1,0:T(8,128)(2,1)S(1)} %get-tuple-element.33), channel_id=1, source_target_pairs={{0,7},{1,6},{2,5},{3,4},{4,3},{5,2},{6,1},{7,0},{8,15},{9,14},{10,... | collective-permute-start | bytes 233480 | tf_op jit(solution)/shard_map/ppermute | solution.py:35
  19.2 10.4 %collective-permute-start.6 = (bf16[304,128]{1,0:T(8,128)(2,1)S(1)}, bf16[304,128]{1,0:T(8,128)(2,1)S(1)}, u32[]{:S(2)}, u32[]{:S(2)}) collective-permute-start(bf16[304,128]{1,0:T(8,128)(2,1)S(1)} %get-tuple-element.34), channel_id=1, source_target_pairs={{0,5},{1,4},{2,7},{3,6},{4,1},{5,0},{6,3},{7,2},{8,13},{9,12},{10,... | collective-permute-start | bytes 233480 | tf_op jit(solution)/shard_map/ppermute | solution.py:35
  20.5 9.1 %collective-permute-start.7 = (bf16[304,128]{1,0:T(8,128)(2,1)S(1)}, bf16[304,128]{1,0:T(8,128)(2,1)S(1)}, u32[]{:S(2)}, u32[]{:S(2)}) collective-permute-start(bf16[304,128]{1,0:T(8,128)(2,1)S(1)} %get-tuple-element.35), channel_id=1, source_target_pairs={{0,2},{1,3},{2,0},{3,1},{4,6},{5,7},{6,4},{7,5},{8,10},{9,11},{10,... | collective-permute-start | bytes 233480 | tf_op jit(solution)/shard_map/ppermute | solution.py:35
  23.4 6.6 %collective-permute-start.8 = (bf16[304,128]{1,0:T(8,128)(2,1)S(1)}, bf16[304,128]{1,0:T(8,128)(2,1)S(1)}, u32[]{:S(2)}, u32[]{:S(2)}) collective-permute-start(bf16[304,128]{1,0:T(8,128)(2,1)S(1)} %get-tuple-element.36), channel_id=1, source_target_pairs={{0,3},{1,2},{2,1},{3,0},{4,7},{5,6},{6,5},{7,4},{8,11},{9,10},{10,... | collective-permute-start | bytes 233480 | tf_op jit(solution)/shard_map/ppermute | solution.py:35
  30.4 8.2 %collective-permute-start.9 = (bf16[288,128]{1,0:T(8,128)(2,1)S(1)}, bf16[288,128]{1,0:T(8,128)(2,1)S(1)}, u32[]{:S(2)}, u32[]{:S(2)}) collective-permute-start(bf16[288,128]{1,0:T(8,128)(2,1)S(1)} %get-tuple-element.38), channel_id=1, source_target_pairs={{0,6},{1,7},{2,4},{3,5},{4,2},{5,3},{6,0},{7,1},{8,14},{9,15},{10,... | collective-permute-start | bytes 221192 | tf_op jit(solution)/shard_map/ppermute | solution.py:35
  33.6 6.2 %collective-permute-start.10 = (bf16[288,128]{1,0:T(8,128)(2,1)S(1)}, bf16[288,128]{1,0:T(8,128)(2,1)S(1)}, u32[]{:S(2)}, u32[]{:S(2)}) collective-permute-start(bf16[288,128]{1,0:T(8,128)(2,1)S(1)} %get-tuple-element.39), channel_id=1, source_target_pairs={{0,1},{1,0},{2,3},{3,2},{4,5},{5,4},{6,7},{7,6},{8,9},{9,8},{10,11... | collective-permute-start | bytes 221192 | tf_op jit(solution)/shard_map/ppermute | solution.py:35
  34.9 7.7 %collective-permute-start.11 = (bf16[288,128]{1,0:T(8,128)(2,1)S(1)}, bf16[288,128]{1,0:T(8,128)(2,1)S(1)}, u32[]{:S(2)}, u32[]{:S(2)}) collective-permute-start(bf16[288,128]{1,0:T(8,128)(2,1)S(1)} %get-tuple-element.40), channel_id=1, source_target_pairs={{0,4},{1,5},{2,6},{3,7},{4,0},{5,1},{6,2},{7,3},{8,12},{9,13},{10,... | collective-permute-start | bytes 221192 | tf_op jit(solution)/shard_map/ppermute | solution.py:35
  34.9 7.7 %collective-permute-start.12 = (bf16[288,128]{1,0:T(8,128)(2,1)S(1)}, bf16[288,128]{1,0:T(8,128)(2,1)S(1)}, u32[]{:S(2)}, u32[]{:S(2)}) collective-permute-start(bf16[288,128]{1,0:T(8,128)(2,1)S(1)} %get-tuple-element.41), channel_id=1, source_target_pairs={{0,7},{1,6},{2,5},{3,4},{4,3},{5,2},{6,1},{7,0},{8,15},{9,14},{10,... | collective-permute-start | bytes 221192 | tf_op jit(solution)/shard_map/ppermute | solution.py:35
  37.1 5.4 %collective-permute-start.14 = (bf16[288,128]{1,0:T(8,128)(2,1)S(1)}, bf16[288,128]{1,0:T(8,128)(2,1)S(1)}, u32[]{:S(2)}, u32[]{:S(2)}) collective-permute-start(bf16[288,128]{1,0:T(8,128)(2,1)S(1)} %get-tuple-element.43), channel_id=1, source_target_pairs={{0,2},{1,3},{2,0},{3,1},{4,6},{5,7},{6,4},{7,5},{8,10},{9,11},{10,... | collective-permute-start | bytes 221192 | tf_op jit(solution)/shard_map/ppermute | solution.py:35
  38.6 5.6 %collective-permute-start.15 = (bf16[288,128]{1,0:T(8,128)(2,1)S(1)}, bf16[288,128]{1,0:T(8,128)(2,1)S(1)}, u32[]{:S(2)}, u32[]{:S(2)}) collective-permute-start(bf16[288,128]{1,0:T(8,128)(2,1)S(1)} %get-tuple-element.44), channel_id=1, source_target_pairs={{0,3},{1,2},{2,1},{3,0},{4,7},{5,6},{6,5},{7,4},{8,11},{9,10},{10,... | collective-permute-start | bytes 221192 | tf_op jit(solution)/shard_map/ppermute | solution.py:35
  39.8 6.6 %collective-permute-start.13 = (bf16[288,128]{1,0:T(8,128)(2,1)S(1)}, bf16[288,128]{1,0:T(8,128)(2,1)S(1)}, u32[]{:S(2)}, u32[]{:S(2)}) collective-permute-start(bf16[288,128]{1,0:T(8,128)(2,1)S(1)} %get-tuple-element.42), channel_id=1, source_target_pairs={{0,5},{1,4},{2,7},{3,6},{4,1},{5,0},{6,3},{7,2},{8,13},{9,12},{10,... | collective-permute-start | bytes 221192 | tf_op jit(solution)/shard_map/ppermute | solution.py:35
  44.2 4.2 %collective-permute-start.16 = (bf16[2,6,16,128]{3,2,1,0:T(8,128)(2,1)S(1)}, bf16[2,6,16,128]{3,2,1,0:T(8,128)(2,1)S(1)}, u32[]{:S(2)}, u32[]{:S(2)}) collective-permute-start(bf16[2,6,16,128]{3,2,1,0:T(8,128)(2,1)S(1)} %get-tuple-element.48), channel_id=1, source_target_pairs={{0,16},{8,24},{16,0},{24,8},{1,17},{9,25},{17,1},{25,9},{2,18},{10... | collective-permute-start | bytes 147464 | tf_op jit(solution)/shard_map/ppermute | solution.py:35
  45.9 3.6 %collective-permute-start.17 = (bf16[2,6,16,128]{3,2,1,0:T(8,128)(2,1)S(1)}, bf16[2,6,16,128]{3,2,1,0:T(8,128)(2,1)S(1)}, u32[]{:S(2)}, u32[]{:S(2)}) collective-permute-start(bf16[2,6,16,128]{3,2,1,0:T(8,128)(2,1)S(1)} %get-tuple-element.49), channel_id=1, source_target_pairs={{0,24},{8,16},{16,8},{24,0},{1,25},{9,17},{17,9},{25,1},{2,26},{10... | collective-permute-start | bytes 147464 | tf_op jit(solution)/shard_map/ppermute | solution.py:35
  45.9 3.6 %collective-permute-start.18 = (bf16[2,6,16,128]{3,2,1,0:T(8,128)(2,1)S(1)}, bf16[2,6,16,128]{3,2,1,0:T(8,128)(2,1)S(1)}, u32[]{:S(2)}, u32[]{:S(2)}) collective-permute-start(bf16[2,6,16,128]{3,2,1,0:T(8,128)(2,1)S(1)} %get-tuple-element.50), channel_id=1, source_target_pairs={{0,8},{8,0},{16,24},{24,16},{1,9},{9,1},{17,25},{25,17},{2,10},{10... | collective-permute-start | bytes 147464 | tf_op jit(solution)/shard_map/ppermute | solution.py:35
  46.4 4.2 %collective-permute-start.19 = (bf16[2,6,16,128]{3,2,1,0:T(8,128)(2,1)S(1)}, bf16[2,6,16,128]{3,2,1,0:T(8,128)(2,1)S(1)}, u32[]{:S(2)}, u32[]{:S(2)}) collective-permute-start(bf16[2,6,16,128]{3,2,1,0:T(8,128)(2,1)S(1)} %get-tuple-element.52), channel_id=1, source_target_pairs={{0,16},{8,24},{16,0},{24,8},{1,17},{9,25},{17,1},{25,9},{2,18},{10... | collective-permute-start | bytes 147464 | tf_op jit(solution)/shard_map/ppermute | solution.py:35
  48.1 3.9 %collective-permute-start.20 = (bf16[2,6,16,128]{3,2,1,0:T(8,128)(2,1)S(1)}, bf16[2,6,16,128]{3,2,1,0:T(8,128)(2,1)S(1)}, u32[]{:S(2)}, u32[]{:S(2)}) collective-permute-start(bf16[2,6,16,128]{3,2,1,0:T(8,128)(2,1)S(1)} %get-tuple-element.53), channel_id=1, source_target_pairs={{0,24},{8,16},{16,8},{24,0},{1,25},{9,17},{17,9},{25,1},{2,26},{10... | collective-permute-start | bytes 147464 | tf_op jit(solution)/shard_map/ppermute | solution.py:35
  48.3 3.8 %collective-permute-start.21 = (bf16[2,6,16,128]{3,2,1,0:T(8,128)(2,1)S(1)}, bf16[2,6,16,128]{3,2,1,0:T(8,128)(2,1)S(1)}, u32[]{:S(2)}, u32[]{:S(2)}) collective-permute-start(bf16[2,6,16,128]{3,2,1,0:T(8,128)(2,1)S(1)} %get-tuple-element.54), channel_id=1, source_target_pairs={{0,8},{8,0},{16,24},{24,16},{1,9},{9,1},{17,25},{25,17},{2,10},{10... | collective-permute-start | bytes 147464 | tf_op jit(solution)/shard_map/ppermute | solution.py:35

commit v2 on v1

--- a/solution.py
+++ b/solution.py
@@ -19,7 +19,7 @@
 
 def start_order(n):
     far = sorted(range(n // 2, n), key=lambda k: (k & 1, -k))
-    return (0, far[0], 1, *far[1:], *range(2, n // 2))
+    return (0, *far[:2], 1, *far[2:], *range(2, n // 2))
 
 
 def my_place():

time: 53 us -> 54.2 us (1.023)
  starting transfers between devices: 32.2 us -> 35.9 us
  waiting for transfers between devices: 11.2 us -> 8.75 us
    ppermute x20, starting transfers between devices: 29 us -> 32.7 us  [all_swapped(): lax.ppermute(part, axis, [(i, i ^ k) for i in range(n)])]
    ppermute x20, waiting for transfers between devices: 10.3 us -> 7.83 us  [all_swapped(): lax.ppermute(part, axis, [(i, i ^ k) for i in range(n)])]
  transfers between devices with their start and end apart: 22 -> 22, of which waited for: 9 -> 8; matrix products, arithmetic and copies ran while one was open for 0% -> 0% of each run, Pallas kernels for 12% -> 12%
where the time goes in v2:
time: 54.2 us; the launch traced here: 54.1 us
  starting transfers between devices  35.9 us (66%)
  waiting for transfers between devices  8.75 us (16%)
  Pallas kernels  7.76 us (14%)
  between operations  1.53 us (3%)
    ppermute x20, starting transfers between devices, all_swapped(): lax.ppermute(part, axis, [(i, i ^ k) for i in range(n)])  32.7 us
    ppermute x20, waiting for transfers between devices, all_swapped(): lax.ppermute(part, axis, [(i, i ^ k) for i in range(n)])  7.83 us
    pallas_call x1, Pallas kernels, edge_proj(): pl.pallas_call(edge_proj_kernel, out_shape=jax.ShapeDtypeStruct((2 * slot...  5.28 us
    ppermute x1, starting transfers between devices, per_device(): left_corner = lax.ppermute(corner, 'site', onward)  2.63 us
  transfers between devices with their start and end apart: 22, of which 8 were waited for; matrix products, arithmetic and copies ran while one was open for 0% of the time, Pallas kernels for 12%

profile of v2, /device:TPU:0, one launch (start us, length us, event | category | flops | bytes accessed | tf_op | source)
XLA Modules:
  0.0 54.1 jit_solution(8126504733775984752)
XLA Ops:
  0.6 0.5 collective-permute-start.1
  1.1 2.6 %collective-permute-start = (bf16[1,6,128,128]{3,2,1,0:T(8,128)(2,1)}, bf16[1,6,128,128]{3,2,1,0:T(8,128)(2,1)S(1)}, u32[]{:S(2)}, u32[]{:S(2)}) collective-permute-start(bf16[1,6,128,128]{3,2,1,0:T(8,128)(2,1)} %param.7), channel_id=1, source_target_pairs={{0,8},{8,16},{16,24},{24,0},{1,9},{9,17},{17,25},{25,1},{2,10},{10... | collective-permute-start | bytes 589832 | tf_op jit(solution)/shard_map/ppermute | solution.py:266
  4.6 5.3 %edge_proj.1.wv = bf16[12,128,128]{2,1,0:T(8,128)(2,1)S(1)} custom-call(bf16[1,6,128,2304]{3,2,1,0:T(8,128)(2,1)} %edge.1, bf16[1,6,128,2304]{3,2,1,0:T(8,128)(2,1)} %bedge.1, bf16[1,6,2304,128]{3,2,1,0:T(8,128)(2,1)} %proj.1), custom_call_target="tpu_custom_call" | custom-call | flops 905969664 | bytes 10616832 | tf_op jit(solution)/shard_map/edge_proj/pallas_call | solution.py:62
  9.9 0.1 pad_maximum_fusion
  10.0 0.9 %collective-permute-done.corner = bf16[1,6,128,128]{3,2,1,0:T(8,128)(2,1)S(1)} collective-permute-done((bf16[1,6,128,128]{3,2,1,0:T(8,128)(2,1)}, bf16[1,6,128,128]{3,2,1,0:T(8,128)(2,1)S(1)}, u32[]{:S(2)}, u32[]{:S(2)}) %collective-permute-start) | collective-permute-done | bytes 196640 | tf_op jit(solution)/shard_map/ppermute | solution.py:266
  10.9 0.0 collective-permute-done.1.bcorner
  10.9 0.1 broadcast_in_dim.2.turn
  10.9 0.5 spread.1
  11.4 4.5 %collective-permute-start.2 = (bf16[304,128]{1,0:T(8,128)(2,1)S(1)}, bf16[304,128]{1,0:T(8,128)(2,1)S(1)}, u32[]{:S(2)}, u32[]{:S(2)}) collective-permute-start(bf16[304,128]{1,0:T(8,128)(2,1)S(1)} %get-tuple-element.30), channel_id=1, source_target_pairs={{0,6},{1,7},{2,4},{3,5},{4,2},{5,3},{6,0},{7,1},{8,14},{9,15},{10,... | collective-permute-start | bytes 233480 | tf_op jit(solution)/shard_map/ppermute | solution.py:35
  15.9 0.0 collective-permute-start.3
  15.9 1.5 %collective-permute-start.4 = (bf16[304,128]{1,0:T(8,128)(2,1)S(1)}, bf16[304,128]{1,0:T(8,128)(2,1)S(1)}, u32[]{:S(2)}, u32[]{:S(2)}) collective-permute-start(bf16[304,128]{1,0:T(8,128)(2,1)S(1)} %get-tuple-element.32), channel_id=1, source_target_pairs={{0,1},{1,0},{2,3},{3,2},{4,5},{5,4},{6,7},{7,6},{8,9},{9,8},{10,11... | collective-permute-start | bytes 233480 | tf_op jit(solution)/shard_map/ppermute | solution.py:35
  17.4 1.9 %collective-permute-start.5 = (bf16[304,128]{1,0:T(8,128)(2,1)S(1)}, bf16[304,128]{1,0:T(8,128)(2,1)S(1)}, u32[]{:S(2)}, u32[]{:S(2)}) collective-permute-start(bf16[304,128]{1,0:T(8,128)(2,1)S(1)} %get-tuple-element.33), channel_id=1, source_target_pairs={{0,7},{1,6},{2,5},{3,4},{4,3},{5,2},{6,1},{7,0},{8,15},{9,14},{10,... | collective-permute-start | bytes 233480 | tf_op jit(solution)/shard_map/ppermute | solution.py:35
  19.2 1.3 %collective-permute-start.6 = (bf16[304,128]{1,0:T(8,128)(2,1)S(1)}, bf16[304,128]{1,0:T(8,128)(2,1)S(1)}, u32[]{:S(2)}, u32[]{:S(2)}) collective-permute-start(bf16[304,128]{1,0:T(8,128)(2,1)S(1)} %get-tuple-element.34), channel_id=1, source_target_pairs={{0,5},{1,4},{2,7},{3,6},{4,1},{5,0},{6,3},{7,2},{8,13},{9,12},{10,... | collective-permute-start | bytes 233480 | tf_op jit(solution)/shard_map/ppermute | solution.py:35
  20.5 0.0 collective-permute-done.2.refs_1_
  20.5 4.1 %collective-permute-start.7 = (bf16[304,128]{1,0:T(8,128)(2,1)S(1)}, bf16[304,128]{1,0:T(8,128)(2,1)S(1)}, u32[]{:S(2)}, u32[]{:S(2)}) collective-permute-start(bf16[304,128]{1,0:T(8,128)(2,1)S(1)} %get-tuple-element.35), channel_id=1, source_target_pairs={{0,2},{1,3},{2,0},{3,1},{4,6},{5,7},{6,4},{7,5},{8,10},{9,11},{10,... | collective-permute-start | bytes 233480 | tf_op jit(solution)/shard_map/ppermute | solution.py:35
  24.6 0.0 collective-permute-done.3.refs_2_
  24.6 2.8 %collective-permute-start.8 = (bf16[304,128]{1,0:T(8,128)(2,1)S(1)}, bf16[304,128]{1,0:T(8,128)(2,1)S(1)}, u32[]{:S(2)}, u32[]{:S(2)}) collective-permute-start(bf16[304,128]{1,0:T(8,128)(2,1)S(1)} %get-tuple-element.36), channel_id=1, source_target_pairs={{0,3},{1,2},{2,1},{3,0},{4,7},{5,6},{6,5},{7,4},{8,11},{9,10},{10,... | collective-permute-start | bytes 233480 | tf_op jit(solution)/shard_map/ppermute | solution.py:35
  27.4 0.0 collective-permute-done.4.refs_3_
  27.4 0.0 collective-permute-done.5.refs_4_
  27.4 2.1 %collective-permute-done.6.refs_5_ = bf16[304,128]{1,0:T(8,128)(2,1)S(1)} collective-permute-done((bf16[304,128]{1,0:T(8,128)(2,1)S(1)}, bf16[304,128]{1,0:T(8,128)(2,1)S(1)}, u32[]{:S(2)}, u32[]{:S(2)}) %collective-permute-start.6) | collective-permute-done | bytes 77856 | tf_op jit(solution)/shard_map/ppermute | solution.py:35
  29.6 0.0 collective-permute-done.7.refs_6_
  29.6 0.9 %collective-permute-done.8.refs_7_ = bf16[304,128]{1,0:T(8,128)(2,1)S(1)} collective-permute-done((bf16[304,128]{1,0:T(8,128)(2,1)S(1)}, bf16[304,128]{1,0:T(8,128)(2,1)S(1)}, u32[]{:S(2)}, u32[]{:S(2)}) %collective-permute-start.8) | collective-permute-done | bytes 77856 | tf_op jit(solution)/shard_map/ppermute | solution.py:35
  30.4 0.3 route.1
  30.8 4.3 %collective-permute-start.9 = (bf16[288,128]{1,0:T(8,128)(2,1)S(1)}, bf16[288,128]{1,0:T(8,128)(2,1)S(1)}, u32[]{:S(2)}, u32[]{:S(2)}) collective-permute-start(bf16[288,128]{1,0:T(8,128)(2,1)S(1)} %get-tuple-element.38), channel_id=1, source_target_pairs={{0,6},{1,7},{2,4},{3,5},{4,2},{5,3},{6,0},{7,1},{8,14},{9,15},{10,... | collective-permute-start | bytes 221192 | tf_op jit(solution)/shard_map/ppermute | solution.py:35
  35.0 0.0 collective-permute-start.10
  35.0 1.5 %collective-permute-start.11 = (bf16[288,128]{1,0:T(8,128)(2,1)S(1)}, bf16[288,128]{1,0:T(8,128)(2,1)S(1)}, u32[]{:S(2)}, u32[]{:S(2)}) collective-permute-start(bf16[288,128]{1,0:T(8,128)(2,1)S(1)} %get-tuple-element.40), channel_id=1, source_target_pairs={{0,1},{1,0},{2,3},{3,2},{4,5},{5,4},{6,7},{7,6},{8,9},{9,8},{10,11... | collective-permute-start | bytes 221192 | tf_op jit(solution)/shard_map/ppermute | solution.py:35
  36.5 1.5 %collective-permute-start.12 = (bf16[288,128]{1,0:T(8,128)(2,1)S(1)}, bf16[288,128]{1,0:T(8,128)(2,1)S(1)}, u32[]{:S(2)}, u32[]{:S(2)}) collective-permute-start(bf16[288,128]{1,0:T(8,128)(2,1)S(1)} %get-tuple-element.41), channel_id=1, source_target_pairs={{0,7},{1,6},{2,5},{3,4},{4,3},{5,2},{6,1},{7,0},{8,15},{9,14},{10,... | collective-permute-start | bytes 221192 | tf_op jit(solution)/shard_map/ppermute | solution.py:35
  38.0 2.0 %collective-permute-start.14 = (bf16[288,128]{1,0:T(8,128)(2,1)S(1)}, bf16[288,128]{1,0:T(8,128)(2,1)S(1)}, u32[]{:S(2)}, u32[]{:S(2)}) collective-permute-start(bf16[288,128]{1,0:T(8,128)(2,1)S(1)} %get-tuple-element.43), channel_id=1, source_target_pairs={{0,2},{1,3},{2,0},{3,1},{4,6},{5,7},{6,4},{7,5},{8,10},{9,11},{10,... | collective-permute-start | bytes 221192 | tf_op jit(solution)/shard_map/ppermute | solution.py:35
  40.0 0.0 collective-permute-done.9.refs_1_.refs_4_.refs_0_
  40.0 2.2 %collective-permute-start.15 = (bf16[288,128]{1,0:T(8,128)(2,1)S(1)}, bf16[288,128]{1,0:T(8,128)(2,1)S(1)}, u32[]{:S(2)}, u32[]{:S(2)}) collective-permute-start(bf16[288,128]{1,0:T(8,128)(2,1)S(1)} %get-tuple-element.44), channel_id=1, source_target_pairs={{0,3},{1,2},{2,1},{3,0},{4,7},{5,6},{6,5},{7,4},{8,11},{9,10},{10,... | collective-permute-start | bytes 221192 | tf_op jit(solution)/shard_map/ppermute | solution.py:35
  42.2 0.0 collective-permute-done.10.refs_2_.refs_5_.refs_1_
  42.2 1.5 %collective-permute-start.13 = (bf16[288,128]{1,0:T(8,128)(2,1)S(1)}, bf16[288,128]{1,0:T(8,128)(2,1)S(1)}, u32[]{:S(2)}, u32[]{:S(2)}) collective-permute-start(bf16[288,128]{1,0:T(8,128)(2,1)S(1)} %get-tuple-element.42), channel_id=1, source_target_pairs={{0,5},{1,4},{2,7},{3,6},{4,1},{5,0},{6,3},{7,2},{8,13},{9,12},{10,... | collective-permute-start | bytes 221192 | tf_op jit(solution)/shard_map/ppermute | solution.py:35
  43.7 0.8 %collective-permute-done.12.refs_4_.refs_6_.refs_2_ = bf16[288,128]{1,0:T(8,128)(2,1)S(1)} collective-permute-done((bf16[288,128]{1,0:T(8,128)(2,1)S(1)}, bf16[288,128]{1,0:T(8,128)(2,1)S(1)}, u32[]{:S(2)}, u32[]{:S(2)}) %collective-permute-start.12) | collective-permute-done | bytes 73760 | tf_op jit(solution)/shard_map/ppermute | solution.py:35
  44.4 0.0 collective-permute-done.14.refs_6_.refs_2_
  44.4 1.5 %collective-permute-done.15.refs_7_.refs_3_ = bf16[288,128]{1,0:T(8,128)(2,1)S(1)} collective-permute-done((bf16[288,128]{1,0:T(8,128)(2,1)S(1)}, bf16[288,128]{1,0:T(8,128)(2,1)S(1)}, u32[]{:S(2)}, u32[]{:S(2)}) %collective-permute-start.15) | collective-permute-done | bytes 73760 | tf_op jit(solution)/shard_map/ppermute | solution.py:35
  46.0 0.1 collective-permute-start.16
  46.1 0.1 collective-permute-start.17
  46.2 2.0 %collective-permute-start.18 = (bf16[2,6,16,128]{3,2,1,0:T(8,128)(2,1)S(1)}, bf16[2,6,16,128]{3,2,1,0:T(8,128)(2,1)S(1)}, u32[]{:S(2)}, u32[]{:S(2)}) collective-permute-start(bf16[2,6,16,128]{3,2,1,0:T(8,128)(2,1)S(1)} %get-tuple-element.50), channel_id=1, source_target_pairs={{0,8},{8,0},{16,24},{24,16},{1,9},{9,1},{17,25},{25,17},{2,10},{10... | collective-permute-start | bytes 147464 | tf_op jit(solution)/shard_map/ppermute | solution.py:35
  48.2 0.9 %collective-permute-done.13.refs_5_.refs_3_ = bf16[288,128]{1,0:T(8,128)(2,1)S(1)} collective-permute-done((bf16[288,128]{1,0:T(8,128)(2,1)S(1)}, bf16[288,128]{1,0:T(8,128)(2,1)S(1)}, u32[]{:S(2)}, u32[]{:S(2)}) %collective-permute-start.13) | collective-permute-done | bytes 73760 | tf_op jit(solution)/shard_map/ppermute | solution.py:35
  49.2 0.1 collective-permute-start.19
  49.2 0.4 collective-permute-start.20
  49.7 0.5 collective-permute-done.16.refs_1_
  50.2 1.2 %collective-permute-start.21 = (bf16[2,6,16,128]{3,2,1,0:T(8,128)(2,1)S(1)}, bf16[2,6,16,128]{3,2,1,0:T(8,128)(2,1)S(1)}, u32[]{:S(2)}, u32[]{:S(2)}) collective-permute-start(bf16[2,6,16,128]{3,2,1,0:T(8,128)(2,1)S(1)} %get-tuple-element.54), channel_id=1, source_target_pairs={{0,8},{8,0},{16,24},{24,16},{1,9},{9,1},{17,25},{25,17},{2,10},{10... | collective-permute-start | bytes 147464 | tf_op jit(solution)/shard_map/ppermute | solution.py:35
  51.4 0.9 %join.1 = (bf16[1,6,128,128]{3,2,1,0:T(8,128)(2,1)}, bf16[2,1,6,128,128]{4,3,2,1,0:T(8,128)(2,1)}) custom-call(bf16[288,128]{1,0:T(8,128)(2,1)S(1)} %get-tuple-element.37.refs_0_, bf16[288,128]{1,0:T(8,128)(2,1)S(1)} %collective-permute-done.9.refs_1_.refs_4_.refs_0_, bf16[288,128]{1,0:T(8,128)(2,1)S(1)} %collective-permute-done.10.refs_2_.refs_5_.refs_1_, ...), custom_call_target="tpu_custom_call" | custom-call | flops 268435456 | bytes 1048576 | tf_op jit(solution)/shard_map/join/pallas_call | solution.py:230
  52.3 0.0 collective-permute-done.17.refs_2_
  52.3 0.0 collective-permute-done.18.refs_3_
  52.3 1.1 %collective-permute-done.19.refs_5_ = bf16[2,6,16,128]{3,2,1,0:T(8,128)(2,1)S(1)} collective-permute-done((bf16[2,6,16,128]{3,2,1,0:T(8,128)(2,1)S(1)}, bf16[2,6,16,128]{3,2,1,0:T(8,128)(2,1)S(1)}, u32[]{:S(2)}, u32[]{:S(2)}) %collective-permute-start.19) | collective-permute-done | bytes 49184 | tf_op jit(solution)/shard_map/ppermute | solution.py:35
  53.3 0.7 %sum.1 = f32[2,6,32,128]{3,2,1,0:T(8,128)} custom-call(bf16[2,6,16,128]{3,2,1,0:T(8,128)(2,1)S(1)} %get-tuple-element.47.refs_0_, bf16[2,6,16,128]{3,2,1,0:T(8,128)(2,1)S(1)} %collective-permute-done.16.refs_1_, bf16[2,6,16,128]{3,2,1,0:T(8,128)(2,1)S(1)} %collective-permute-done.17.refs_2_, bf16[2,6,16,128]{3,2,1,0:T(8,128)(2,1)S(1)} %collective-permute-done.18.refs_3_, ...), custom_call_target="tpu_custom_call" | custom-call | flops 268435456 | bytes 1048576 | tf_op jit(solution)/shard_map/sum/pallas_call | solution.py:233
  (7 shorter events, 0.1 us)
Async XLA Ops:
  0.6 10.2 %collective-permute-start.1 = (bf16[2,1,6,128,128]{4,3,2,1,0:T(8,128)(2,1)}, bf16[2,1,6,128,128]{4,3,2,1,0:T(8,128)(2,1)S(1)}, u32[]{:S(2)}, u32[]{:S(2)}) collective-permute-start(bf16[2,1,6,128,128]{4,3,2,1,0:T(8,128)(2,1)} %param.8), channel_id=1, source_target_pairs={{0,8},{8,16},{16,24},{24,0},{1,9},{9,17},{17,25},{25,1},{2,10},{10... | collective-permute-start | bytes 1179656 | tf_op jit(solution)/shard_map/ppermute | solution.py:265
  1.1 9.7 %collective-permute-start = (bf16[1,6,128,128]{3,2,1,0:T(8,128)(2,1)}, bf16[1,6,128,128]{3,2,1,0:T(8,128)(2,1)S(1)}, u32[]{:S(2)}, u32[]{:S(2)}) collective-permute-start(bf16[1,6,128,128]{3,2,1,0:T(8,128)(2,1)} %param.7), channel_id=1, source_target_pairs={{0,8},{8,16},{16,24},{24,0},{1,9},{9,17},{17,25},{25,1},{2,10},{10... | collective-permute-start | bytes 589832 | tf_op jit(solution)/shard_map/ppermute | solution.py:266
  4.6 25.9 %copy-start = (s32[1,48]{1,0:T(1,128)S(1)}, s32[1,48]{1,0:T(1,128)}, u32[]{:S(2)}) copy-start(s32[1,48]{1,0:T(1,128)} %joining.1) | copy-start | bytes 580
  11.4 9.1 %collective-permute-start.2 = (bf16[304,128]{1,0:T(8,128)(2,1)S(1)}, bf16[304,128]{1,0:T(8,128)(2,1)S(1)}, u32[]{:S(2)}, u32[]{:S(2)}) collective-permute-start(bf16[304,128]{1,0:T(8,128)(2,1)S(1)} %get-tuple-element.30), channel_id=1, source_target_pairs={{0,6},{1,7},{2,4},{3,5},{4,2},{5,3},{6,0},{7,1},{8,14},{9,15},{10,... | collective-permute-start | bytes 233480 | tf_op jit(solution)/shard_map/ppermute | solution.py:35
  15.9 8.8 %collective-permute-start.3 = (bf16[304,128]{1,0:T(8,128)(2,1)S(1)}, bf16[304,128]{1,0:T(8,128)(2,1)S(1)}, u32[]{:S(2)}, u32[]{:S(2)}) collective-permute-start(bf16[304,128]{1,0:T(8,128)(2,1)S(1)} %get-tuple-element.31), channel_id=1, source_target_pairs={{0,4},{1,5},{2,6},{3,7},{4,0},{5,1},{6,2},{7,3},{8,12},{9,13},{10,... | collective-permute-start | bytes 233480 | tf_op jit(solution)/shard_map/ppermute | solution.py:35
  15.9 11.5 %collective-permute-start.4 = (bf16[304,128]{1,0:T(8,128)(2,1)S(1)}, bf16[304,128]{1,0:T(8,128)(2,1)S(1)}, u32[]{:S(2)}, u32[]{:S(2)}) collective-permute-start(bf16[304,128]{1,0:T(8,128)(2,1)S(1)} %get-tuple-element.32), channel_id=1, source_target_pairs={{0,1},{1,0},{2,3},{3,2},{4,5},{5,4},{6,7},{7,6},{8,9},{9,8},{10,11... | collective-permute-start | bytes 233480 | tf_op jit(solution)/shard_map/ppermute | solution.py:35
  17.4 10.1 %collective-permute-start.5 = (bf16[304,128]{1,0:T(8,128)(2,1)S(1)}, bf16[304,128]{1,0:T(8,128)(2,1)S(1)}, u32[]{:S(2)}, u32[]{:S(2)}) collective-permute-start(bf16[304,128]{1,0:T(8,128)(2,1)S(1)} %get-tuple-element.33), channel_id=1, source_target_pairs={{0,7},{1,6},{2,5},{3,4},{4,3},{5,2},{6,1},{7,0},{8,15},{9,14},{10,... | collective-permute-start | bytes 233480 | tf_op jit(solution)/shard_map/ppermute | solution.py:35
  19.2 10.3 %collective-permute-start.6 = (bf16[304,128]{1,0:T(8,128)(2,1)S(1)}, bf16[304,128]{1,0:T(8,128)(2,1)S(1)}, u32[]{:S(2)}, u32[]{:S(2)}) collective-permute-start(bf16[304,128]{1,0:T(8,128)(2,1)S(1)} %get-tuple-element.34), channel_id=1, source_target_pairs={{0,5},{1,4},{2,7},{3,6},{4,1},{5,0},{6,3},{7,2},{8,13},{9,12},{10,... | collective-permute-start | bytes 233480 | tf_op jit(solution)/shard_map/ppermute | solution.py:35
  20.5 9.0 %collective-permute-start.7 = (bf16[304,128]{1,0:T(8,128)(2,1)S(1)}, bf16[304,128]{1,0:T(8,128)(2,1)S(1)}, u32[]{:S(2)}, u32[]{:S(2)}) collective-permute-start(bf16[304,128]{1,0:T(8,128)(2,1)S(1)} %get-tuple-element.35), channel_id=1, source_target_pairs={{0,2},{1,3},{2,0},{3,1},{4,6},{5,7},{6,4},{7,5},{8,10},{9,11},{10,... | collective-permute-start | bytes 233480 | tf_op jit(solution)/shard_map/ppermute | solution.py:35
  24.6 5.8 %collective-permute-start.8 = (bf16[304,128]{1,0:T(8,128)(2,1)S(1)}, bf16[304,128]{1,0:T(8,128)(2,1)S(1)}, u32[]{:S(2)}, u32[]{:S(2)}) collective-permute-start(bf16[304,128]{1,0:T(8,128)(2,1)S(1)} %get-tuple-element.36), channel_id=1, source_target_pairs={{0,3},{1,2},{2,1},{3,0},{4,7},{5,6},{6,5},{7,4},{8,11},{9,10},{10,... | collective-permute-start | bytes 233480 | tf_op jit(solution)/shard_map/ppermute | solution.py:35
  30.8 9.2 %collective-permute-start.9 = (bf16[288,128]{1,0:T(8,128)(2,1)S(1)}, bf16[288,128]{1,0:T(8,128)(2,1)S(1)}, u32[]{:S(2)}, u32[]{:S(2)}) collective-permute-start(bf16[288,128]{1,0:T(8,128)(2,1)S(1)} %get-tuple-element.38), channel_id=1, source_target_pairs={{0,6},{1,7},{2,4},{3,5},{4,2},{5,3},{6,0},{7,1},{8,14},{9,15},{10,... | collective-permute-start | bytes 221192 | tf_op jit(solution)/shard_map/ppermute | solution.py:35
  35.0 7.1 %collective-permute-start.10 = (bf16[288,128]{1,0:T(8,128)(2,1)S(1)}, bf16[288,128]{1,0:T(8,128)(2,1)S(1)}, u32[]{:S(2)}, u32[]{:S(2)}) collective-permute-start(bf16[288,128]{1,0:T(8,128)(2,1)S(1)} %get-tuple-element.39), channel_id=1, source_target_pairs={{0,4},{1,5},{2,6},{3,7},{4,0},{5,1},{6,2},{7,3},{8,12},{9,13},{10,... | collective-permute-start | bytes 221192 | tf_op jit(solution)/shard_map/ppermute | solution.py:35
  35.0 8.6 %collective-permute-start.11 = (bf16[288,128]{1,0:T(8,128)(2,1)S(1)}, bf16[288,128]{1,0:T(8,128)(2,1)S(1)}, u32[]{:S(2)}, u32[]{:S(2)}) collective-permute-start(bf16[288,128]{1,0:T(8,128)(2,1)S(1)} %get-tuple-element.40), channel_id=1, source_target_pairs={{0,1},{1,0},{2,3},{3,2},{4,5},{5,4},{6,7},{7,6},{8,9},{9,8},{10,11... | collective-permute-start | bytes 221192 | tf_op jit(solution)/shard_map/ppermute | solution.py:35
  36.5 7.9 %collective-permute-start.12 = (bf16[288,128]{1,0:T(8,128)(2,1)S(1)}, bf16[288,128]{1,0:T(8,128)(2,1)S(1)}, u32[]{:S(2)}, u32[]{:S(2)}) collective-permute-start(bf16[288,128]{1,0:T(8,128)(2,1)S(1)} %get-tuple-element.41), channel_id=1, source_target_pairs={{0,7},{1,6},{2,5},{3,4},{4,3},{5,2},{6,1},{7,0},{8,15},{9,14},{10,... | collective-permute-start | bytes 221192 | tf_op jit(solution)/shard_map/ppermute | solution.py:35
  38.0 6.4 %collective-permute-start.14 = (bf16[288,128]{1,0:T(8,128)(2,1)S(1)}, bf16[288,128]{1,0:T(8,128)(2,1)S(1)}, u32[]{:S(2)}, u32[]{:S(2)}) collective-permute-start(bf16[288,128]{1,0:T(8,128)(2,1)S(1)} %get-tuple-element.43), channel_id=1, source_target_pairs={{0,2},{1,3},{2,0},{3,1},{4,6},{5,7},{6,4},{7,5},{8,10},{9,11},{10,... | collective-permute-start | bytes 221192 | tf_op jit(solution)/shard_map/ppermute | solution.py:35
  40.0 6.0 %collective-permute-start.15 = (bf16[288,128]{1,0:T(8,128)(2,1)S(1)}, bf16[288,128]{1,0:T(8,128)(2,1)S(1)}, u32[]{:S(2)}, u32[]{:S(2)}) collective-permute-start(bf16[288,128]{1,0:T(8,128)(2,1)S(1)} %get-tuple-element.44), channel_id=1, source_target_pairs={{0,3},{1,2},{2,1},{3,0},{4,7},{5,6},{6,5},{7,4},{8,11},{9,10},{10,... | collective-permute-start | bytes 221192 | tf_op jit(solution)/shard_map/ppermute | solution.py:35
  42.2 6.9 %collective-permute-start.13 = (bf16[288,128]{1,0:T(8,128)(2,1)S(1)}, bf16[288,128]{1,0:T(8,128)(2,1)S(1)}, u32[]{:S(2)}, u32[]{:S(2)}) collective-permute-start(bf16[288,128]{1,0:T(8,128)(2,1)S(1)} %get-tuple-element.42), channel_id=1, source_target_pairs={{0,5},{1,4},{2,7},{3,6},{4,1},{5,0},{6,3},{7,2},{8,13},{9,12},{10,... | collective-permute-start | bytes 221192 | tf_op jit(solution)/shard_map/ppermute | solution.py:35
  46.0 4.2 %collective-permute-start.16 = (bf16[2,6,16,128]{3,2,1,0:T(8,128)(2,1)S(1)}, bf16[2,6,16,128]{3,2,1,0:T(8,128)(2,1)S(1)}, u32[]{:S(2)}, u32[]{:S(2)}) collective-permute-start(bf16[2,6,16,128]{3,2,1,0:T(8,128)(2,1)S(1)} %get-tuple-element.48), channel_id=1, source_target_pairs={{0,16},{8,24},{16,0},{24,8},{1,17},{9,25},{17,1},{25,9},{2,18},{10... | collective-permute-start | bytes 147464 | tf_op jit(solution)/shard_map/ppermute | solution.py:35
  46.1 6.2 %collective-permute-start.17 = (bf16[2,6,16,128]{3,2,1,0:T(8,128)(2,1)S(1)}, bf16[2,6,16,128]{3,2,1,0:T(8,128)(2,1)S(1)}, u32[]{:S(2)}, u32[]{:S(2)}) collective-permute-start(bf16[2,6,16,128]{3,2,1,0:T(8,128)(2,1)S(1)} %get-tuple-element.49), channel_id=1, source_target_pairs={{0,24},{8,16},{16,8},{24,0},{1,25},{9,17},{17,9},{25,1},{2,26},{10... | collective-permute-start | bytes 147464 | tf_op jit(solution)/shard_map/ppermute | solution.py:35
  46.2 6.1 %collective-permute-start.18 = (bf16[2,6,16,128]{3,2,1,0:T(8,128)(2,1)S(1)}, bf16[2,6,16,128]{3,2,1,0:T(8,128)(2,1)S(1)}, u32[]{:S(2)}, u32[]{:S(2)}) collective-permute-start(bf16[2,6,16,128]{3,2,1,0:T(8,128)(2,1)S(1)} %get-tuple-element.50), channel_id=1, source_target_pairs={{0,8},{8,0},{16,24},{24,16},{1,9},{9,1},{17,25},{25,17},{2,10},{10... | collective-permute-start | bytes 147464 | tf_op jit(solution)/shard_map/ppermute | solution.py:35
  49.2 4.2 %collective-permute-start.19 = (bf16[2,6,16,128]{3,2,1,0:T(8,128)(2,1)S(1)}, bf16[2,6,16,128]{3,2,1,0:T(8,128)(2,1)S(1)}, u32[]{:S(2)}, u32[]{:S(2)}) collective-permute-start(bf16[2,6,16,128]{3,2,1,0:T(8,128)(2,1)S(1)} %get-tuple-element.52), channel_id=1, source_target_pairs={{0,16},{8,24},{16,0},{24,8},{1,17},{9,25},{17,1},{25,9},{2,18},{10... | collective-permute-start | bytes 147464 | tf_op jit(solution)/shard_map/ppermute | solution.py:35
  49.2 4.1 %collective-permute-start.20 = (bf16[2,6,16,128]{3,2,1,0:T(8,128)(2,1)S(1)}, bf16[2,6,16,128]{3,2,1,0:T(8,128)(2,1)S(1)}, u32[]{:S(2)}, u32[]{:S(2)}) collective-permute-start(bf16[2,6,16,128]{3,2,1,0:T(8,128)(2,1)S(1)} %get-tuple-element.53), channel_id=1, source_target_pairs={{0,24},{8,16},{16,8},{24,0},{1,25},{9,17},{17,9},{25,1},{2,26},{10... | collective-permute-start | bytes 147464 | tf_op jit(solution)/shard_map/ppermute | solution.py:35
  50.2 3.2 %collective-permute-start.21 = (bf16[2,6,16,128]{3,2,1,0:T(8,128)(2,1)S(1)}, bf16[2,6,16,128]{3,2,1,0:T(8,128)(2,1)S(1)}, u32[]{:S(2)}, u32[]{:S(2)}) collective-permute-start(bf16[2,6,16,128]{3,2,1,0:T(8,128)(2,1)S(1)} %get-tuple-element.54), channel_id=1, source_target_pairs={{0,8},{8,0},{16,24},{24,16},{1,9},{9,1},{17,25},{25,17},{2,10},{10... | collective-permute-start | bytes 147464 | tf_op jit(solution)/shard_map/ppermute | solution.py:35
